TPU v7x, 32 devices: a whole 2x2x4 slice. The times are simulated.
32 devices in a mesh: dp: 8 (over z, y), tensor: 4 (over x, core).
Axes of the slice: x: 2, y: 2, z: 4, core: 2. Of those that a mesh axis runs over, the one named last changes fastest.
Arguments:
- tokens: bfloat16 [4096, 768], P('dp'), may hold values from -6 to 6
- cotangent: bfloat16 [4096, 768], P('dp'), may hold values from -6 to 6
- gain_attn: float32 [768], replicated, may hold values from 0.5 to 1.5
- w_qkv: bfloat16 [768, 2304], P(None, 'tensor'), may hold values from -0.21875 to 0.21875
- w_out: bfloat16 [768, 768], P('tensor'), may hold values from -1.75 to 1.75
- gain_ffn: float32 [768], replicated, may hold values from 0.5 to 1.5
- w_router: bfloat16 [768, 16], replicated, may hold values from -0.15625 to 0.15625
- w_shared_gate: bfloat16 [768, 2048], P(None, 'tensor'), may hold values from -0.21875 to 0.21875
- w_shared_up: bfloat16 [768, 2048], P(None, 'tensor'), may hold values from -0.21875 to 0.21875
- w_shared_down: bfloat16 [2048, 768], P('tensor'), may hold values from -0.125 to 0.125
- routed_gate_weight: bfloat16 [768, 32768], P(None, ('dp', 'tensor')), may hold values from -0.21875 to 0.21875
- routed_up_weight: bfloat16 [768, 32768], P(None, ('dp', 'tensor')), may hold values from -0.21875 to 0.21875
- w_expert_down: bfloat16 [32768, 768], P(('dp', 'tensor')), may hold values from -0.125 to 0.125
- seq_lengths: int32 [8, 8], P('dp'), may hold values from 0 to 512, as said below
- token_order: int32 [4096], P('dp'), may hold values from 0 to 4095, as said below
- inverse_order: int32 [4096], P('dp'), may hold values from 0 to 4095, as said below
- routes: int32 [4096, 2], P('dp'), may hold values from 0 to 15, all different within a row; in each aligned block of 512 rows (0 to 511, 512 to 1023, ...) at most 128 rows name the same one
- fill_order: int32 [8, 1024], P('dp'), may hold values from 0 to 1023, each once within a row
Outputs:
- out: bfloat16 [4096, 768], P('dp')
- grad_tokens: bfloat16 [4096, 768], P('dp')
- grad_gain_attn: float32 [768], P('dp')
- grad_w_qkv: float32 [768, 2304], P('dp', 'tensor')
- grad_w_out: float32 [768, 768], P('tensor', 'dp')
- grad_gain_ffn: float32 [768], P('dp')
- grad_w_router: float32 [768, 16], P('dp')
- grad_w_shared_gate: float32 [768, 2048], P('dp', 'tensor')
- grad_w_shared_up: float32 [768, 2048], P('dp', 'tensor')
- grad_w_shared_down: float32 [2048, 768], P('tensor', 'dp')
- grad_w_expert_gate: float32 [768, 32768], P(None, ('dp', 'tensor'))
- routed_up_weight_gradient: float32 [768, 32768], P(None, ('dp', 'tensor'))
- grad_w_expert_down: float32 [32768, 768], P(('dp', 'tensor'))
Inputs may be any that keep to these rules, and one draw needn't show every extreme that they name: `token_order`: each block of 512 balanced positions takes the same number of tokens from every block of 512 initial positions, and the tokens that go from one such block to another keep their order. The inverse of token_order: token_order[inverse_order[t]] = t. `seq_lengths`: each row sums to 512; a zero is an unused entry; some row is one sequence of 512 tokens. `routes`: A row names two different experts; in the rows of one block of 512 balanced positions no expert is named more than 128 times, a bound that some block reaches. `fill_order`: each row is a permutation of its block's pair indices.
All inputs are finite; a program needn't handle non-finite values.
Results may differ from a plain program's by a relative error of at most 0.014.
The roundings to bfloat16 on the way count: a program that leaves them out, or rounds other values in their place, can miss the bound.
Values may be sent and summed in bfloat16 or wider, within the bound.
No kernel may reach another device: no remote copies, remote signals or barrier semaphores. Data moves between devices by JAX's collectives and lax.ppermute only.
A program may use at most 256 MiB of HBM per device.

v0:
```python
import jax
import jax.numpy as jnp
from jax import lax
from jax.sharding import PartitionSpec as P

HD = 64


epsilon = 1e-06


def rope_tables(positions, head_size):
    half_size = head_size // 2
    exponent = jnp.arange(half_size, dtype=jnp.float32) * (-2.0 / head_size)
    inverse_freq = jnp.power(10000.0, exponent)
    angles = positions.astype(jnp.float32)[:, None] * inverse_freq[None, :]
    return (jnp.cos(angles), jnp.sin(angles))


def rope_turn(values, cosine, sine):
    half_size = values.shape[-1] // 2
    first_half = values[..., :half_size]
    second_half = values[..., half_size:]
    return jnp.concatenate(
        [first_half * cosine - second_half * sine, second_half * cosine + first_half * sine], -1
    )


def rope_back(grads, cosine, sine):
    half_size = grads.shape[-1] // 2
    first_half = grads[..., :half_size]
    second_half = grads[..., half_size:]
    return jnp.concatenate(
        [first_half * cosine + second_half * sine, second_half * cosine - first_half * sine], -1
    )


def segment_layout(lengths_row, row_count):
    seq_ends = jnp.cumsum(lengths_row)
    local_places = jnp.arange(row_count, dtype=jnp.int32)
    passed = local_places[:, None] >= seq_ends[None, :]
    segment = jnp.sum(passed.astype(jnp.int32), 1)
    seq_start = jnp.max(jnp.where(passed, seq_ends[None, :], 0), 1)
    return (segment, local_places - seq_start)


def rms_forward(values, gain):
    inverse_root = lax.rsqrt(jnp.mean(values * values, -1, keepdims=True) + epsilon)
    return (values * inverse_root * gain, inverse_root)


def rms_backward(values, inverse_root, gain, grad_normed):
    scaled = grad_normed * gain
    grad_values = inverse_root * scaled - values * inverse_root**3 * jnp.mean(
        scaled * values, -1, keepdims=True
    )
    grad_gain = jnp.sum(grad_normed * values * inverse_root, 0)
    return (grad_values, grad_gain)


def silu_parts(gate_in):
    sigmoid_val = jax.nn.sigmoid(gate_in)
    return (gate_in * sigmoid_val, sigmoid_val * (1.0 + gate_in * (1.0 - sigmoid_val)))


def weight_gradient(left, right):
    return lax.dot_general(
        left, right, (((0,), (0,)), ((), ())), preferred_element_type=jnp.float32
    )


def backward_product(grads, weight):
    return lax.dot_general(
        grads, weight, (((1,), (1,)), ((), ())), preferred_element_type=jnp.float32
    )


def block_mask(segment, first_row, rows_block):
    row_count = segment.shape[0]
    key_places = jnp.arange(row_count, dtype=jnp.int32)
    row_places = first_row + jnp.arange(rows_block, dtype=jnp.int32)
    return (segment[:, None] == segment[None, :]) & (key_places[None, :] <= row_places[:, None])


def attend_forward(query, keys, values, segment, score_scale):
    row_count = query.shape[0]
    rows_block = min(512, row_count)

    def one_block(block_id):
        first_row = block_id * rows_block
        allowed = block_mask(segment, first_row, rows_block)
        scores = (
            jnp.einsum("qhd,khd->hqk", query, keys, preferred_element_type=jnp.float32)
            * score_scale
        )
        scores = jnp.where(allowed[None], scores, -1e30)
        top_score = jnp.max(scores, -1, keepdims=True)
        exponent_vals = jnp.exp(scores - top_score)
        row_total = jnp.sum(exponent_vals, -1, keepdims=True)
        weights = (exponent_vals / row_total).astype(jnp.bfloat16)
        mixed = jnp.einsum("hqk,khd->qhd", weights, values, preferred_element_type=jnp.float32)
        return (mixed, (top_score + jnp.log(row_total))[:, :, 0])

    mixed, log_total = lax.map(one_block, jnp.arange(row_count // rows_block, dtype=jnp.int32))
    return (mixed.reshape(row_count, query.shape[1], query.shape[2]), log_total)


def attend_backward(query, keys, values, segment, score_scale, log_total, grad_mixed):
    row_count = query.shape[0]
    rows_block = min(512, row_count)

    def one_block(carry, block_id):
        first_row = block_id * rows_block
        allowed = block_mask(segment, first_row, rows_block)
        scores = (
            jnp.einsum("qhd,khd->hqk", query, keys, preferred_element_type=jnp.float32)
            * score_scale
        )
        scores = jnp.where(allowed[None], scores, -1e30)
        weights = jnp.where(allowed[None], jnp.exp(scores - log_total[block_id][:, :, None]), 0.0)
        grad_weights = jnp.einsum(
            "qhd,khd->hqk", grad_mixed, values, preferred_element_type=jnp.float32
        )
        row_delta = jnp.sum(weights * grad_weights, -1, keepdims=True)
        grad_scores = (weights * (grad_weights - row_delta)).astype(jnp.bfloat16)
        grad_query = (
            jnp.einsum("hqk,khd->qhd", grad_scores, keys, preferred_element_type=jnp.float32)
            * score_scale
        )
        grad_keys = (
            carry[0]
            + jnp.einsum("hqk,qhd->khd", grad_scores, query, preferred_element_type=jnp.float32)
            * score_scale
        )
        grad_values = carry[1] + jnp.einsum(
            "hqk,qhd->khd",
            weights.astype(jnp.bfloat16),
            grad_mixed,
            preferred_element_type=jnp.float32,
        )
        return ((grad_keys, grad_values), grad_query)

    zeros_keys = jnp.zeros(keys.shape, jnp.float32)
    sums, grad_query = lax.scan(
        one_block, (zeros_keys, zeros_keys), jnp.arange(row_count // rows_block, dtype=jnp.int32)
    )
    return (grad_query.reshape(query.shape), sums[0], sums[1])


def expert_layout(experts_all):
    devices_dp = lax.axis_size("dp")
    groups_tensor = lax.axis_size("tensor")
    per_dp = max(1, experts_all // devices_dp)
    copies = max(1, devices_dp // experts_all)
    local_pick = lax.axis_index("tensor") // (groups_tensor // per_dp)
    return (devices_dp, per_dp, copies, local_pick)


def spread_targets(values, devices_dp, per_dp, copies):
    tail = values.shape[1:]
    grouped = values.reshape((devices_dp // copies, 1, per_dp) + tail)
    widened = jnp.broadcast_to(grouped, (devices_dp // copies, copies, per_dp) + tail)
    return widened.reshape((devices_dp, per_dp) + tail)


def to_experts(rows, counts, layout, capacity):
    devices_dp, per_dp, copies, local_pick = layout
    slot_rows = rows.shape[1]
    width = rows.shape[2]
    sent_rows = spread_targets(rows, devices_dp, per_dp, copies)
    sent_counts = spread_targets(counts, devices_dp, per_dp, copies)
    got_rows, got_counts = (
        lax.all_to_all(sent_rows, "dp", split_axis=0, concat_axis=0, tiled=True),
        lax.all_to_all(sent_counts, "dp", split_axis=0, concat_axis=0, tiled=True),
    )
    chosen_rows = lax.dynamic_index_in_dim(got_rows, local_pick, 1, keepdims=False)
    arrived = lax.dynamic_index_in_dim(got_counts, local_pick, 1, keepdims=False)
    earlier = jnp.cumsum(arrived) - arrived
    slot_places = jnp.arange(slot_rows, dtype=jnp.int32)
    kept = (slot_places[None, :] < arrived[:, None]) & (
        earlier[:, None] + slot_places[None, :] < capacity
    )
    return (chosen_rows.reshape(devices_dp * slot_rows, width), kept.reshape(-1, 1))


def from_experts(rows, devices_dp):
    returned = lax.all_to_all(
        rows.reshape(devices_dp, -1, rows.shape[-1]), "dp", split_axis=0, concat_axis=0, tiled=True
    )
    return returned.reshape(-1, rows.shape[-1])


def pair_collect(returned, pair_slot, slot_rows, layout):
    devices_dp, per_dp, copies, local_pick = layout
    expert_of = pair_slot // slot_rows
    rank_of = pair_slot % slot_rows
    first_target = expert_of // per_dp * copies
    total = jnp.zeros(pair_slot.shape + (returned.shape[-1],), jnp.float32)
    for replica in range(copies):
        total = total + returned[(first_target + replica) * slot_rows + rank_of].astype(jnp.float32)
    match = expert_of % per_dp == local_pick
    return jnp.where(match[:, :, None], total, 0.0)


def on_device(
    tokens,
    cotangent,
    gain_attn,
    w_qkv,
    w_out,
    gain_ffn,
    w_router,
    w_shared_gate,
    w_shared_up,
    w_shared_down,
    routed_gate_weight,
    routed_up_weight,
    w_expert_down,
    seq_lengths,
    token_order,
    inverse_order,
    routes,
    fill_order,
):
    devices_dp = lax.axis_size("dp")
    row_count, width = tokens.shape
    block_rows = row_count // devices_dp
    experts_all = w_router.shape[1]
    slot_rows = 4 * row_count // experts_all
    capacity = 5 * row_count * devices_dp // (2 * experts_all)
    head_size = HD
    heads_local = w_out.shape[0] // head_size
    brain_float = jnp.bfloat16
    layout = expert_layout(experts_all)
    by_target = jnp.argsort(inverse_order)
    by_anchor = jnp.argsort(token_order)
    to_balanced = jnp.argsort(by_anchor)
    to_anchor = jnp.argsort(by_target)
    sent_tokens = tokens[by_target].reshape(devices_dp, block_rows, width)
    sent_cotangent = cotangent[by_target].reshape(devices_dp, block_rows, width)
    got_tokens, got_cotangent = (
        lax.all_to_all(sent_tokens, "dp", split_axis=0, concat_axis=0, tiled=True),
        lax.all_to_all(sent_cotangent, "dp", split_axis=0, concat_axis=0, tiled=True),
    )
    balanced = got_tokens.reshape(row_count, width)[to_balanced].astype(jnp.float32)
    grad_out = got_cotangent.reshape(row_count, width)[to_balanced].astype(jnp.float32)
    segment, position = segment_layout(seq_lengths[0], row_count)
    cosine, sine = rope_tables(position, head_size)
    cosine = cosine[:, None, :]
    sine = sine[:, None, :]
    normed_attn, root_attn = rms_forward(balanced, gain_attn)
    normed_attn_low = normed_attn.astype(brain_float)
    projected = jnp.dot(normed_attn_low, w_qkv, preferred_element_type=jnp.float32).reshape(
        row_count, heads_local, 3, head_size
    )
    query = rope_turn(projected[:, :, 0], cosine, sine).astype(brain_float)
    keys = rope_turn(projected[:, :, 1], cosine, sine).astype(brain_float)
    values = projected[:, :, 2].astype(brain_float)
    score_scale = head_size ** (-0.5)
    mixed, log_total = attend_forward(query, keys, values, segment, score_scale)
    mixed_low = mixed.reshape(row_count, heads_local * head_size).astype(brain_float)
    attn_part = jnp.dot(mixed_low, w_out, preferred_element_type=jnp.float32)
    attn_total = lax.psum(attn_part, "tensor")
    after_attn = balanced + attn_total
    normed_ffn, root_ffn = rms_forward(after_attn, gain_ffn)
    normed_low = normed_ffn.astype(brain_float)
    logits = jnp.dot(normed_low, w_router, preferred_element_type=jnp.float32)
    gates = jax.nn.softmax(jnp.take_along_axis(logits, routes, 1), -1)
    shared_gate = jnp.dot(normed_low, w_shared_gate, preferred_element_type=jnp.float32)
    shared_up = jnp.dot(normed_low, w_shared_up, preferred_element_type=jnp.float32)
    shared_act, shared_slope = silu_parts(shared_gate)
    shared_hidden = (shared_act * shared_up).astype(brain_float)
    shared_part = jnp.dot(shared_hidden, w_shared_down, preferred_element_type=jnp.float32)
    fill_row = fill_order[0]
    pair_expert = routes.reshape(-1)[fill_row]
    expert_ids = jnp.arange(experts_all, dtype=jnp.int32)
    member = (pair_expert[:, None] == expert_ids[None, :]).astype(jnp.int32)
    pair_rank = jnp.sum(jnp.cumsum(member, 0) * member, 1) - 1
    counts = jnp.sum(member, 0)
    slot_index = pair_expert * slot_rows + pair_rank
    slot_pair = jnp.zeros(experts_all * slot_rows, jnp.int32).at[slot_index].set(fill_row)
    pair_slot = (
        jnp.zeros(2 * row_count, jnp.int32).at[fill_row].set(slot_index).reshape(row_count, 2)
    )
    sent_rows = normed_low[slot_pair // 2].reshape(experts_all, slot_rows, width)
    expert_token_rows, kept = to_experts(sent_rows, counts, layout, capacity)
    expert_gate = jnp.dot(expert_token_rows, routed_gate_weight, preferred_element_type=jnp.float32)
    expert_up = jnp.dot(expert_token_rows, routed_up_weight, preferred_element_type=jnp.float32)
    expert_act, expert_slope = silu_parts(expert_gate)
    expert_hidden = (expert_act * expert_up).astype(brain_float)
    expert_part = jnp.dot(expert_hidden, w_expert_down, preferred_element_type=jnp.float32).astype(
        brain_float
    )
    expert_part = jnp.where(kept, expert_part, jnp.zeros((), brain_float))
    returned = from_experts(expert_part, devices_dp)
    pair_rows = pair_collect(returned, pair_slot, slot_rows, layout)
    ffn_part = shared_part + jnp.sum(gates[:, :, None] * pair_rows, 1)
    ffn_total = lax.psum(ffn_part.astype(jnp.bfloat16), "tensor").astype(jnp.float32)
    result = after_attn + ffn_total
    grad_low = grad_out.astype(brain_float)
    grad_w_shared_down = weight_gradient(shared_hidden, grad_low)
    shared_hidden_grad = backward_product(grad_low, w_shared_down)
    grad_sgate = (shared_hidden_grad * shared_up * shared_slope).astype(brain_float)
    grad_sup = (shared_hidden_grad * shared_act).astype(brain_float)
    grad_w_shared_gate = weight_gradient(normed_low, grad_sgate)
    grad_w_shared_up = weight_gradient(normed_low, grad_sup)
    normed_grad = backward_product(grad_sgate, w_shared_gate) + backward_product(
        grad_sup, w_shared_up
    )
    pair_grads = (
        (gates[:, :, None] * grad_out[:, None, :]).astype(brain_float).reshape(2 * row_count, width)
    )
    sent_grads = pair_grads[slot_pair].reshape(experts_all, slot_rows, width)
    expert_grads, kept_back = to_experts(sent_grads, counts, layout, capacity)
    expert_grads = jnp.where(kept_back, expert_grads, jnp.zeros((), brain_float))
    gate_grad_part = jnp.sum(pair_rows * grad_out[:, None, :], 2)
    again_up, recomputed_activation, again_slope, again_hidden = (
        expert_up,
        expert_act,
        expert_slope,
        expert_hidden,
    )
    grad_w_expert_down = weight_gradient(again_hidden, expert_grads)
    expert_hidden_gradient = backward_product(expert_grads, w_expert_down)
    expert_gate_gradient = (expert_hidden_gradient * again_up * again_slope).astype(brain_float)
    expert_up_gradient = (expert_hidden_gradient * recomputed_activation).astype(brain_float)
    grad_w_expert_gate = weight_gradient(expert_token_rows, expert_gate_gradient)
    routed_up_weight_gradient = weight_gradient(expert_token_rows, expert_up_gradient)
    row_gradients = (
        backward_product(expert_gate_gradient, routed_gate_weight)
        + backward_product(expert_up_gradient, routed_up_weight)
    ).astype(brain_float)
    grad_back = from_experts(row_gradients, devices_dp)
    normed_grad = normed_grad + jnp.sum(pair_collect(grad_back, pair_slot, slot_rows, layout), 1)
    normed_grad, gate_grad = lax.psum((normed_grad, gate_grad_part), "tensor")
    weighted = jnp.sum(gates * gate_grad, 1, keepdims=True)
    chosen_grad = gates * (gate_grad - weighted)
    route_match = (routes[:, :, None] == expert_ids[None, None, :]).astype(jnp.float32)
    logit_grad = jnp.sum(route_match * chosen_grad[:, :, None], 1).astype(brain_float)
    grad_w_router = weight_gradient(normed_low, logit_grad)
    normed_grad = normed_grad + backward_product(logit_grad, w_router)
    after_grad, grad_gain_ffn = rms_backward(after_attn, root_ffn, gain_ffn, normed_grad)
    after_grad = after_grad + grad_out
    after_grad_low = after_grad.astype(brain_float)
    grad_w_out = weight_gradient(mixed_low, after_grad_low)
    mixed_grad = (
        backward_product(after_grad_low, w_out)
        .astype(brain_float)
        .reshape(row_count, heads_local, head_size)
    )
    query_grad, key_grad, value_grad = attend_backward(
        query, keys, values, segment, score_scale, log_total, mixed_grad
    )
    projected_grad = jnp.stack(
        [rope_back(query_grad, cosine, sine), rope_back(key_grad, cosine, sine), value_grad], 2
    )
    projected_grad = projected_grad.astype(brain_float).reshape(
        row_count, heads_local * 3 * head_size
    )
    grad_w_qkv = weight_gradient(normed_attn_low, projected_grad)
    attn_normed_grad = lax.psum(backward_product(projected_grad, w_qkv), "tensor")
    input_grad, grad_gain_attn = rms_backward(balanced, root_attn, gain_attn, attn_normed_grad)
    input_grad = input_grad + after_grad
    summed = (
        lax.psum_scatter(grad_gain_attn, "dp", scatter_dimension=0, tiled=True),
        lax.psum_scatter(grad_w_qkv, "dp", scatter_dimension=0, tiled=True),
        lax.psum_scatter(grad_w_out, "dp", scatter_dimension=1, tiled=True),
        lax.psum_scatter(grad_gain_ffn, "dp", scatter_dimension=0, tiled=True),
        lax.psum_scatter(grad_w_router, "dp", scatter_dimension=0, tiled=True),
        lax.psum_scatter(grad_w_shared_gate, "dp", scatter_dimension=0, tiled=True),
        lax.psum_scatter(grad_w_shared_up, "dp", scatter_dimension=0, tiled=True),
        lax.psum_scatter(grad_w_shared_down, "dp", scatter_dimension=1, tiled=True),
    )
    sent_result = result.astype(brain_float)[by_anchor].reshape(devices_dp, block_rows, width)
    sent_input = input_grad.astype(brain_float)[by_anchor].reshape(devices_dp, block_rows, width)
    got_result, got_input = (
        lax.all_to_all(sent_result, "dp", split_axis=0, concat_axis=0, tiled=True),
        lax.all_to_all(sent_input, "dp", split_axis=0, concat_axis=0, tiled=True),
    )
    final = got_result.reshape(row_count, width)[to_anchor]
    grad_tokens = got_input.reshape(row_count, width)[to_anchor]
    return (
        final,
        grad_tokens,
        summed[0],
        summed[1],
        summed[2],
        summed[3],
        summed[4],
        summed[5],
        summed[6],
        summed[7],
        grad_w_expert_gate,
        routed_up_weight_gradient,
        grad_w_expert_down,
    )


def solution(mesh):
    return jax.shard_map(
        on_device,
        mesh=mesh,
        in_specs=(
            P("dp", None),
            P("dp", None),
            P(),
            P(None, "tensor"),
            P("tensor", None),
            P(),
            P(),
            P(None, "tensor"),
            P(None, "tensor"),
            P("tensor", None),
            P(None, ("dp", "tensor")),
            P(None, ("dp", "tensor")),
            P(("dp", "tensor"), None),
            P("dp", None),
            P("dp"),
            P("dp"),
            P("dp", None),
            P("dp", None),
        ),
        out_specs=(
            P("dp", None),
            P("dp", None),
            P("dp"),
            P("dp", "tensor"),
            P("tensor", "dp"),
            P("dp"),
            P("dp", None),
            P("dp", "tensor"),
            P("dp", "tensor"),
            P("tensor", "dp"),
            P(None, ("dp", "tensor")),
            P(None, ("dp", "tensor")),
            P(("dp", "tensor"), None),
        ),
        check_vma=False,
    )
```

profile of v0, /device:TPU:0, one launch (start us, length us, event | category | flops | bytes accessed | tf_op | source)
XLA Modules:
  0.0 944.5 jit_solution(17300104356139004028)
XLA Ops:
  7.2 4.6 sort.59
  12.4 4.3 gather_fusion
  16.7 7.4 all-to-all-start
  25.1 4.5 gather_fusion.2
  29.9 4.5 reduce-window.27
  34.7 3.8 sort.60
  38.5 3.8 sort.61
  55.5 5.3 all-to-all-start.1
  60.8 2.7 gather_fusion.7
  63.5 3.7 all-to-all-done.1
  67.2 3.6 all-to-all-start.5
  70.8 4.5 scatter_custom_fusion.1
  75.3 23.1 %all-reduce.8.cloned.1.call-done = f32[512,768]{1,0:T(8,128)} async-done(((f32[512,768]{1,0:T(8,128)}), f32[512,768]{1,0:T(8,128)}) %all-reduce.8.cloned.1.call-update) | async-done | bytes 1572880 | tf_op jit(solution)/shard_map/psum | solution.py:263
  101.5 9.4 gather_fusion.3
  110.9 5.9 all-to-all-start.2
  117.1 2.7 gather_fusion.8
  119.9 3.6 mul.439
  123.5 5.3 mul.440
  129.0 8.7 gather_fusion.13
  138.4 3.3 multiply_convert_fusion.4
  141.7 11.7 %gather_fusion.9 = bf16[2048,768]{1,0:T(8,128)(2,1)} fusion(bf16[1024,768]{1,0:T(8,128)(2,1)} %multiply_convert_fusion.4, s32[2048]{0:T(1024)S(1)} %get-tuple-element.111), kind=kCustom, calls=%fused_computation.9 | custom fusion | bytes 6299648 | tf_op jit(solution)/shard_map/gather | solution.py:313
  153.4 34.0 %all-to-all-done.2 = bf16[8,2,128,768]{3,2,1,0:T(8,128)(2,1)} async-done(((bf16[8,2,128,768]{3,2,1,0:T(8,128)(2,1)}), bf16[8,2,128,768]{3,2,1,0:T(8,128)(2,1)}, u32[]{:S(2)}, u32[]{:S(2)}) %all-to-all-start.2) | async-done | bytes 3145760 | tf_op jit(solution)/shard_map/all_to_all | solution.py:173
  187.4 4.5 all-to-all-start.6
  194.4 3.8 fusion.73
  198.1 3.7 fusion.74
  201.9 60.2 %all-to-all-done.6 = bf16[8,2,128,768]{3,2,1,0:T(8,128)(2,1)} async-done(((bf16[8,2,128,768]{3,2,1,0:T(8,128)(2,1)}), bf16[8,2,128,768]{3,2,1,0:T(8,128)(2,1)}, u32[]{:S(2)}, u32[]{:S(2)}) %all-to-all-start.6) | async-done | bytes 3145760 | tf_op jit(solution)/shard_map/all_to_all | solution.py:173
  264.7 6.8 multiply_convert_fusion
  274.2 3.0 add_convert_fusion
  277.2 4.3 all-to-all-start.7
  281.5 4.5 broadcast_select_fusion.1
  286.0 32.1 %all-to-all-done.7 = bf16[8,128,768]{2,1,0:T(8,128)(2,1)} async-done(((bf16[8,128,768]{2,1,0:T(8,128)(2,1)}), bf16[8,128,768]{2,1,0:T(8,128)(2,1)}, u32[]{:S(2)}, u32[]{:S(2)}) %all-to-all-start.7) | async-done | bytes 1572896 | tf_op jit(solution)/shard_map/all_to_all | solution.py:187
  318.1 4.3 all-to-all-start.3
  322.5 4.7 scatter_custom_fusion
  340.7 7.2 gather_fusion.10
  347.9 4.9 reshape.796
  352.7 6.3 all-to-all-done.3
  359.0 7.2 gather_fusion.4
  366.2 4.9 reshape.795
  371.1 20.1 %multiply_reduce_fusion.1 = (f32[512,2]{1,0:T(8,128)S(1)}, f32[512,768]{1,0:T(8,128)}, f32[512,768]{1,0:T(8,128)S(1)}) fusion(f32[512,2,768]{2,1,0:T(2,128)} %reshape.795, pred[512,2]{1,0:T(8,128)(4,1)S(1)} %copy.139, f32[512,768]{1,0:T(8,128)} %convert_element_type.143, f32[512,2]{1,0:T(8,128)S(1)} %copy.131, f32[512,2,768]{2,1,0:T(2,128)} %reshape.796), kind=kLoop, calls=%fused_computation.29 | loop fusion | flops 4717568 | bytes 11019264 | tf_op jit(solution)/shard_map/reduce_sum | solution.py:316
  393.8 5.7 psum.38
  399.6 3.1 add_convert_fusion.2
  403.0 31.5 %all-reduce.12.cloned.1.call-done = f32[512,768]{1,0:T(8,128)} async-done(((f32[512,768]{1,0:T(8,128)}), f32[512,768]{1,0:T(8,128)}) %all-reduce.12.cloned.1.call-update) | async-done | bytes 1572880 | tf_op jit(solution)/shard_map/psum | solution.py:335
  434.5 3.6 multiply_reduce_fusion.3
  438.1 34.0 %all-reduce.10.cloned.1.call-done = bf16[512,768]{1,0:T(8,128)(2,1)} async-done(((bf16[512,768]{1,0:T(8,128)(2,1)}), bf16[512,768]{1,0:T(8,128)(2,1)}) %all-reduce.10.cloned.1.call-update) | async-done | bytes 786448 | tf_op jit(solution)/shard_map/psum | solution.py:298
  472.1 3.0 subtract_add_fusion
  487.0 2.8 convolution_bitcast_fusion
  489.8 2.9 fusion.78
  492.8 2.8 fusion.79
  495.7 3.2 fusion.80
  499.0 3.3 fusion.29
  505.7 5.9 all-to-all-start.4
  511.7 3.8 sort.62
  516.7 12.8 %all-reduce.14.cloned.1.call-done = f32[512,768]{1,0:T(8,128)} async-done(((f32[512,768]{1,0:T(8,128)}), f32[512,768]{1,0:T(8,128)}) %all-reduce.14.cloned.1.call-update) | async-done | bytes 1572880 | tf_op jit(solution)/shard_map/psum | solution.py:361
  536.3 5.9 all-to-all-start.8
  542.2 5.7 fusion.83
  548.0 3.5 fusion.81
  551.5 3.5 fusion.82
  555.0 43.8 %reduce-scatter.21.cloned.1.call-done = f32[96,16]{1,0:T(8,128)} async-done(((f32[768,16]{1,0:T(8,128)}), f32[96,16]{1,0:T(8,128)}) %reduce-scatter.21.cloned.1.call-update) | async-done | bytes 6160
  600.2 19.9 %all-reduce.2 = (f32[768]{0:T(1024)S(1)}, f32[768]{0:T(1024)S(1)}) all-reduce(f32[768]{0:T(1024)S(1)} %get-tuple-element.76, f32[768]{0:T(1024)S(1)} %get-tuple-element.74), channel_id=2, replica_groups=mesh['dp'=8,'tensor'=4] {'dp'}, use_global_device_ids=true, to_apply=%region_34.35.clone | all-reduce | flops 1536 | bytes 12288
  621.3 42.2 %reduce-scatter.19.cloned.1.call-done = f32[96,192]{1,0:T(8,128)} async-done(((f32[768,192]{1,0:T(8,128)}), f32[96,192]{1,0:T(8,128)}) %reduce-scatter.19.cloned.1.call-update) | async-done | bytes 73744
  670.5 61.2 %reduce-scatter.13.cloned.1.call-done = f32[96,512]{1,0:T(8,128)} async-done(((f32[768,512]{1,0:T(8,128)}), f32[96,512]{1,0:T(8,128)}) %reduce-scatter.13.cloned.1.call-update) | async-done | bytes 196624 | tf_op jit(solution)/shard_map/reduce_scatter | solution.py:370
  731.7 67.8 %reduce-scatter.15.cloned.1.call-done = f32[96,512]{1,0:T(8,128)} async-done(((f32[768,512]{1,0:T(8,128)}), f32[96,512]{1,0:T(8,128)}) %reduce-scatter.15.cloned.1.call-update) | async-done | bytes 196624 | tf_op jit(solution)/shard_map/reduce_scatter | solution.py:371
  799.4 68.1 %reduce-scatter.17.cloned.1.call-done = f32[512,96]{0,1:T(8,128)} async-done(((f32[512,768]{0,1:T(8,128)}), f32[512,96]{0,1:T(8,128)}) %reduce-scatter.17.cloned.1.call-update) | async-done | bytes 196624 | tf_op jit(solution)/shard_map/reduce_scatter | solution.py:372
  867.6 69.7 %reduce-scatter.11.cloned.1.call-done = f32[96,576]{1,0:T(8,128)} async-done(((f32[768,576]{1,0:T(8,128)}), f32[96,576]{1,0:T(8,128)}) %reduce-scatter.11.cloned.1.call-update) | async-done | bytes 221200 | tf_op jit(solution)/shard_map/reduce_scatter | solution.py:366
  (302 shorter events, 75.8 us)
Async XLA Ops:
  7.2 256.9 %copy-start = (bf16[1024,768]{1,0:T(8,128)(2,1)S(1)}, bf16[1024,768]{1,0:T(8,128)(2,1)}, u32[]{:S(2)}) copy-start(bf16[1024,768]{1,0:T(8,128)(2,1)} %param.30) | copy-start | bytes 4718596
  12.4 4.3 copy-start.65
  16.7 7.5 copy-start.73
  16.7 8.1 copy-start.51
  16.7 27.6 %all-to-all-start = ((bf16[8,64,768]{2,1,0:T(8,128)(2,1)}), bf16[8,64,768]{2,1,0:T(8,128)(2,1)S(1)}, u32[]{:S(2)}, u32[]{:S(2)}) async-start(bf16[8,64,768]{2,1,0:T(8,128)(2,1)} %bitcast), calls=%async_computation | async-start | bytes 1572864 | tf_op jit(solution)/shard_map/all_to_all | solution.py:242
  24.1 74.2 %all-reduce.8.cloned.1.call-start = ((), (), s32[]{:S(2)}) async-start(), calls=%async_computation.15 | async-start | bytes 3145728 | tf_op jit(solution)/shard_map/psum | solution.py:263
  25.1 4.6 copy-start.79
  25.1 9.6 %copy-start.74 = (s32[512]{0:T(512)S(1)}, s32[512]{0:T(512)}, u32[]{:S(2)}) copy-start(s32[512]{0:T(512)} %param.32) | copy-start | bytes 6148
  38.5 3.8 copy-start.71
  42.7 6.6 copy-start.36
  42.7 6.6 copy-start.38
  43.6 7.4 copy-start.20
  44.3 2.9 copy-start.54
  46.3 2.8 copy-start.2
  53.0 7.8 copy-start.1
  53.0 7.8 copy-start.66
  55.5 11.7 %all-to-all-start.1 = ((s32[8,1,2]{2,1,0:T(1,128)}), s32[8,1,2]{2,1,0:T(1,128)S(1)}, u32[]{:S(2)}, u32[]{:S(2)}) async-start(s32[8,1,2]{2,1,0:T(1,128)} %bitcast.16), calls=%async_computation.1 | async-start | bytes 8192 | tf_op jit(solution)/shard_map/all_to_all | solution.py:174
  63.5 34.9 %copy-start.3 = (bf16[512,768]{1,0:T(8,128)(2,1)S(1)}, bf16[512,768]{1,0:T(8,128)(2,1)}, u32[]{:S(2)}) copy-start(bf16[512,768]{1,0:T(8,128)(2,1)} %copy-done.2) | copy-start | bytes 2359300
  67.2 43.7 %all-to-all-start.5 = ((bf16[8,64,768]{2,1,0:T(8,128)(2,1)}), bf16[8,64,768]{2,1,0:T(8,128)(2,1)S(1)}, u32[]{:S(2)}, u32[]{:S(2)}) async-start(bf16[8,64,768]{2,1,0:T(8,128)(2,1)} %bitcast.153), calls=%async_computation.5 | async-start | bytes 1572864 | tf_op jit(solution)/shard_map/all_to_all | solution.py:243
  75.3 26.0 %copy-start.52 = (f32[768]{0:T(1024)S(1)}, f32[768]{0:T(1024)}, u32[]{:S(2)}) copy-start(f32[768]{0:T(1024)} %param.23) | copy-start | bytes 9220
  100.6 10.2 %copy-start.62 = (f32[512]{0:T(512)}, f32[512]{0:T(512)S(1)}, u32[]{:S(2)}) copy-start(f32[512]{0:T(512)S(1)} %get-tuple-element.118) | copy-start | bytes 6148
  110.9 76.5 %all-to-all-start.2 = ((bf16[8,2,128,768]{3,2,1,0:T(8,128)(2,1)}), bf16[8,2,128,768]{3,2,1,0:T(8,128)(2,1)}, u32[]{:S(2)}, u32[]{:S(2)}) async-start(bf16[8,2,128,768]{3,2,1,0:T(8,128)(2,1)} %bitcast.148), calls=%async_computation.2 | async-start | bytes 6291456 | tf_op jit(solution)/shard_map/all_to_all | solution.py:173
  123.5 5.3 copy-start.50
  187.4 74.7 %all-to-all-start.6 = ((bf16[8,2,128,768]{3,2,1,0:T(8,128)(2,1)}), bf16[8,2,128,768]{3,2,1,0:T(8,128)(2,1)}, u32[]{:S(2)}, u32[]{:S(2)}) async-start(bf16[8,2,128,768]{3,2,1,0:T(8,128)(2,1)} %bitcast.147), calls=%async_computation.6 | async-start | bytes 6291456 | tf_op jit(solution)/shard_map/all_to_all | solution.py:173
  194.1 4.0 copy-start.11
  194.4 3.8 copy-start.77
  262.1 2.7 copy-start.81
  264.7 6.8 copy-start.29
  264.7 6.8 copy-start.76
  271.6 2.6 copy-start.78
  277.2 40.9 %all-to-all-start.7 = ((bf16[8,128,768]{2,1,0:T(8,128)(2,1)}), bf16[8,128,768]{2,1,0:T(8,128)(2,1)}, u32[]{:S(2)}, u32[]{:S(2)}) async-start(bf16[8,128,768]{2,1,0:T(8,128)(2,1)} %bitcast.155), calls=%async_computation.7 | async-start | bytes 3145728 | tf_op jit(solution)/shard_map/all_to_all | solution.py:187
  318.1 40.9 %all-to-all-start.3 = ((bf16[8,128,768]{2,1,0:T(8,128)(2,1)}), bf16[8,128,768]{2,1,0:T(8,128)(2,1)}, u32[]{:S(2)}, u32[]{:S(2)}) async-start(bf16[8,128,768]{2,1,0:T(8,128)(2,1)} %bitcast.154), calls=%async_computation.3 | async-start | bytes 3145728 | tf_op jit(solution)/shard_map/all_to_all | solution.py:187
  322.4 11.0 %copy-start.10 = (bf16[512,768]{1,0:T(8,128)(2,1)S(1)}, bf16[512,768]{1,0:T(8,128)(2,1)}, u32[]{:S(2)}) copy-start(bf16[512,768]{1,0:T(8,128)(2,1)} %gather_fusion.8) | copy-start | bytes 2359300
  322.4 112.0 %all-reduce.12.cloned.1.call-start = ((), (), s32[]{:S(2)}) async-start(), calls=%async_computation.17 | async-start | bytes 3145728 | tf_op jit(solution)/shard_map/psum | solution.py:335
  371.1 20.1 %copy-start.15 = (f32[512,768]{1,0:T(8,128)S(1)}, f32[512,768]{1,0:T(8,128)}, u32[]{:S(2)}) copy-start(f32[512,768]{1,0:T(8,128)} %fusion.75) | copy-start | bytes 4718596
  371.1 20.1 %copy-start.19 = (bf16[768,512]{1,0:T(8,128)(2,1)S(1)}, bf16[768,512]{1,0:T(8,128)(2,1)}, u32[]{:S(2)}) copy-start(bf16[768,512]{1,0:T(8,128)(2,1)} %param.26) | copy-start | bytes 2359300
  371.1 20.1 %copy-start.27 = (bf16[512,512]{1,0:T(8,128)(2,1)S(1)}, bf16[512,512]{1,0:T(8,128)(2,1)}, u32[]{:S(2)}) copy-start(bf16[512,512]{1,0:T(8,128)(2,1)} %get-tuple-element.92) | copy-start | bytes 1572868
  393.0 6.6 copy-start.26
  393.0 79.1 %all-reduce.10.cloned.1.call-start = ((), (), s32[]{:S(2)}) async-start(), calls=%async_computation.16 | async-start | bytes 1572864 | tf_op jit(solution)/shard_map/psum | solution.py:298
  399.6 34.9 %copy-start.53 = (f32[768]{0:T(1024)S(1)}, f32[768]{0:T(1024)}, u32[]{:S(2)}) copy-start(f32[768]{0:T(1024)} %param.23) | copy-start | bytes 9220
  399.6 34.9 %copy-start.63 = (f32[512]{0:T(512)S(1)}, f32[512]{0:T(512)}, u32[]{:S(2)}) copy-start(f32[512]{0:T(512)} %copy-done.62) | copy-start | bytes 6148
  402.7 69.4 %copy-start.68 = (f32[512]{0:T(512)S(1)}, f32[512]{0:T(512)}, u32[]{:S(2)}) copy-start(f32[512]{0:T(512)} %get-tuple-element.117) | copy-start | bytes 6148
  402.7 126.8 %all-reduce.14.cloned.1.call-start = ((), (), s32[]{:S(2)}) async-start(), calls=%async_computation.18 | async-start | bytes 3145728 | tf_op jit(solution)/shard_map/psum | solution.py:361
  472.1 3.0 copy-start.31
  472.1 3.4 copy-start.14
  475.1 3.5 copy-start.8
  485.7 113.1 %reduce-scatter.21.cloned.1.call-start = ((), (), s32[]{:S(2)}) async-start(), calls=%async_computation.24 | async-start | bytes 442368
  486.9 176.5 %reduce-scatter.19.cloned.1.call-start = ((), (), s32[]{:S(2)}) async-start(), calls=%async_computation.23 | async-start | bytes 884736
  489.8 241.9 %reduce-scatter.13.cloned.1.call-start = ((), (), s32[]{:S(2)}) async-start(), calls=%async_computation.20 | async-start | bytes 1769472 | tf_op jit(solution)/shard_map/reduce_scatter | solution.py:370
  492.7 306.7 %reduce-scatter.15.cloned.1.call-start = ((), (), s32[]{:S(2)}) async-start(), calls=%async_computation.21 | async-start | bytes 1769472 | tf_op jit(solution)/shard_map/reduce_scatter | solution.py:371
  495.6 3.4 copy-start.4
  495.6 3.4 copy-start.55
  495.6 3.4 copy-start.61
  495.7 371.9 %reduce-scatter.17.cloned.1.call-start = ((), (), s32[]{:S(2)}) async-start(), calls=%async_computation.22 | async-start | bytes 1769472 | tf_op jit(solution)/shard_map/reduce_scatter | solution.py:372
  498.9 438.3 %reduce-scatter.11.cloned.1.call-start = ((), (), s32[]{:S(2)}) async-start(), calls=%async_computation.19 | async-start | bytes 2211840 | tf_op jit(solution)/shard_map/reduce_scatter | solution.py:366
  505.7 6.0 copy-start.70
  505.7 9.8 %copy-start.80 = (u32[32]{0:T(128)S(1)}, u32[32]{0:T(128)}, u32[]{:S(2)}) copy-start(u32[32]{0:T(128)} %constant.221) | copy-start | bytes 388
  505.7 23.8 %copy-start.5 = (bf16[512,768]{1,0:T(8,128)(2,1)S(1)}, bf16[512,768]{1,0:T(8,128)(2,1)}, u32[]{:S(2)}) copy-start(bf16[512,768]{1,0:T(8,128)(2,1)} %copy-done.2) | copy-start | bytes 2359300
  505.7 30.6 %all-to-all-start.4 = ((bf16[8,64,768]{2,1,0:T(8,128)(2,1)}), bf16[8,64,768]{2,1,0:T(8,128)(2,1)S(1)}, u32[]{:S(2)}, u32[]{:S(2)}) async-start(bf16[8,64,768]{2,1,0:T(8,128)(2,1)} %bitcast.151), calls=%async_computation.4 | async-start | bytes 1572864 | tf_op jit(solution)/shard_map/all_to_all | solution.py:377
  511.7 20.0 %copy-start.67 = (f32[512]{0:T(512)S(1)}, f32[512]{0:T(512)}, u32[]{:S(2)}) copy-start(f32[512]{0:T(512)} %get-tuple-element.115) | copy-start | bytes 6148
  536.3 131.5 %all-to-all-start.8 = ((bf16[8,64,768]{2,1,0:T(8,128)(2,1)}), bf16[8,64,768]{2,1,0:T(8,128)(2,1)S(1)}, u32[]{:S(2)}, u32[]{:S(2)}) async-start(bf16[8,64,768]{2,1,0:T(8,128)(2,1)} %bitcast.152), calls=%async_computation.8 | async-start | bytes 1572864 | tf_op jit(solution)/shard_map/all_to_all | solution.py:378
  542.2 5.7 copy-start.12
  542.2 5.7 copy-start.25
  548.0 3.5 copy-start.23
  (37 other events, 46.8 us)
Sparse Core Ops, SparseCore 0:
  54.7 43.5 all-reduce.7
  393.1 41.2 all-reduce.11
  437.4 34.6 all-reduce.9
  485.8 43.7 all-reduce.13
  532.7 66.0 reduce-scatter.20
  601.9 61.5 reduce-scatter.18
  667.8 63.7 reduce-scatter.12
  735.7 63.7 reduce-scatter.14
  803.8 63.6 reduce-scatter.16
  871.5 65.7 reduce-scatter.10
where the time goes:
time: 955 us; the launch traced here: 944 us
  waiting for transfers between devices  591 us (62%)
  local copies, waits for them, and re-layouts  125 us (13%)
  matrix products  78.2 us (8%)
  other arithmetic  60 us (6%)
  starting transfers between devices  47.7 us (5%)
  blocking collectives  25.6 us (3%)
  between operations  16.5 us (2%)
    all_to_all x2, waiting for transfers between devices, to_experts(): lax.all_to_all(sent_rows, 'dp', split_axis=0, concat_axis=0, tiled=True)  94.2 us
    unnamed x12, waiting for transfers between devices  86.1 us
    reduce_scatter x1, waiting for transfers between devices, on_device(): lax.psum_scatter(grad_w_qkv, 'dp', scatter_dimension=0, tiled=True)  69.7 us
    reduce_scatter x1, waiting for transfers between devices, on_device(): lax.psum_scatter(grad_w_shared_down, 'dp', scatter_dimension=1, tiled=True)  68.1 us
    reduce_scatter x1, waiting for transfers between devices, on_device(): lax.psum_scatter(grad_w_shared_up, 'dp', scatter_dimension=0, tiled=True)  67.8 us
    reduce_scatter x1, waiting for transfers between devices, on_device(): lax.psum_scatter(grad_w_shared_gate, 'dp', scatter_dimension=0, tiled=True)  61.2 us
    all_to_all x2, waiting for transfers between devices, from_experts(): lax.all_to_all(rows.reshape(devices_dp, -1, rows.shape[-1]), 'dp', split_...  38.4 us
    psum x1, waiting for transfers between devices, on_device(): lax.psum(ffn_part.astype(jnp.bfloat16), 'tensor').astype(jnp.float32)  34 us
  transfers between devices with their start and end apart: 19, of which 16 were waited for; matrix products, arithmetic and copies ran while one was open for 19% of the time, Pallas kernels for 0%

commit v1 on v0

v1 whole, which is shorter than its diff:
```python
import jax
import jax.numpy as jnp
from jax import lax
from jax.sharding import Mesh, PartitionSpec as P

HD = 64
EPSILON = 1e-06
BF = jnp.bfloat16
F32 = jnp.float32
DP = ("dz", "dy")
TP = ("hi", "lo")


def dot(left, right):
    return jnp.dot(left, right, preferred_element_type=F32)


def dot_t(left, right):
    return lax.dot_general(left, right, (((0,), (0,)), ((), ())), preferred_element_type=F32)


def dot_bt(left, right):
    return lax.dot_general(left, right, (((1,), (1,)), ((), ())), preferred_element_type=F32)


def swap(values, axis):
    return lax.ppermute(values, axis, [(0, 1), (1, 0)])


def gather_rel(values, axes):
    for axis in axes:
        values = jnp.concatenate([values, swap(values, axis)], 0)
    return values


def exchange(values):
    return lax.all_to_all(values, DP, split_axis=0, concat_axis=0, tiled=True)


def scatter_dp(grads):
    dz, dy = lax.axis_size("dz"), lax.axis_size("dy")
    my_z, my_y = lax.axis_index("dz"), lax.axis_index("dy")
    chunk = grads.shape[0] // (dz * dy)
    columns = grads.shape[1]
    view = grads.reshape(dz, dy, chunk, columns)
    keep = lax.dynamic_index_in_dim(view, my_y, 1, keepdims=False)
    send = lax.dynamic_index_in_dim(view, 1 - my_y, 1, keepdims=False).astype(BF)
    keep = keep + swap(send, "dy").astype(F32)
    step = 1
    while step < dz:
        view = keep.reshape(-1, 2, chunk, columns)
        bit = (my_z // step) % 2
        send = lax.dynamic_index_in_dim(view, 1 - bit, 1, keepdims=False).astype(BF)
        keep = lax.dynamic_index_in_dim(view, bit, 1, keepdims=False)
        got = lax.ppermute(send, "dz", [(i, i ^ step) for i in range(dz)])
        keep = keep + got.astype(F32)
        step *= 2
    return keep.reshape(chunk, columns)


def rope_tables(positions, head_size):
    half_size = head_size // 2
    exponent = jnp.arange(half_size, dtype=F32) * (-2.0 / head_size)
    inverse_freq = jnp.power(10000.0, exponent)
    angles = positions.astype(F32)[:, None] * inverse_freq[None, :]
    return (jnp.cos(angles), jnp.sin(angles))


def rope_turn(values, cosine, sine):
    half_size = values.shape[-1] // 2
    first_half = values[..., :half_size]
    second_half = values[..., half_size:]
    return jnp.concatenate(
        [first_half * cosine - second_half * sine, second_half * cosine + first_half * sine], -1
    )


def rope_back(grads, cosine, sine):
    half_size = grads.shape[-1] // 2
    first_half = grads[..., :half_size]
    second_half = grads[..., half_size:]
    return jnp.concatenate(
        [first_half * cosine + second_half * sine, second_half * cosine - first_half * sine], -1
    )


def segment_layout(lengths_row, row_count):
    seq_ends = jnp.cumsum(lengths_row)
    local_places = jnp.arange(row_count, dtype=jnp.int32)
    passed = local_places[:, None] >= seq_ends[None, :]
    segment = jnp.sum(passed.astype(jnp.int32), 1)
    seq_start = jnp.max(jnp.where(passed, seq_ends[None, :], 0), 1)
    return (segment, local_places - seq_start)


def inverse_root(values):
    return lax.rsqrt(jnp.mean(values * values, -1, keepdims=True) + EPSILON)


def rms_backward(values, root, gain, grad_normed):
    scaled = grad_normed * gain
    return root * scaled - values * root**3 * jnp.mean(scaled * values, -1, keepdims=True)


def silu_parts(gate_in):
    sigmoid_val = jax.nn.sigmoid(gate_in)
    return (gate_in * sigmoid_val, sigmoid_val * (1.0 + gate_in * (1.0 - sigmoid_val)))


def bucket_rank(buckets, bucket_count):
    count = buckets.shape[0]
    member = (buckets[:, None] == jnp.arange(bucket_count, dtype=jnp.int32)[None, :]).astype(BF)
    places = jnp.arange(count, dtype=jnp.int32)
    earlier = (places[None, :] < places[:, None]).astype(BF)
    return jnp.sum(dot(earlier, member) * member.astype(F32), 1).astype(jnp.int32)


def on_device(
    tokens,
    cotangent,
    gain_attn,
    w_qkv,
    w_out,
    gain_ffn,
    w_router,
    w_shared_gate,
    w_shared_up,
    w_shared_down,
    routed_gate_weight,
    routed_up_weight,
    w_expert_down,
    seq_lengths,
    token_order,
    inverse_order,
    routes,
    fill_order,
):
    devices_dp = lax.axis_size(DP)
    devices_tp = lax.axis_size(TP)
    row_count, width = tokens.shape
    block_rows = row_count // devices_dp
    shard_block = block_rows // devices_tp
    shard_rows = row_count // devices_tp
    half_rows = row_count // 2
    experts_all = w_router.shape[1]
    slot_rows = 4 * row_count // experts_all
    capacity = 5 * row_count * devices_dp // (2 * experts_all)
    heads = w_out.shape[0] // HD
    per_dp = max(1, experts_all // devices_dp)
    copies = max(1, devices_dp // experts_all)
    sub_axes = ("lo",) if per_dp == 2 else TP
    sub = devices_tp // per_dp
    my_hi, my_lo = lax.axis_index("hi"), lax.axis_index("lo")
    my_dp = lax.axis_index(DP)
    my_block = my_lo * 2 + my_hi
    pick = my_hi if per_dp == 2 else 0
    my_part = my_lo if per_dp == 2 else my_block
    part_rows = slot_rows // sub
    my_expert = my_dp // copies * per_dp + pick
    ints = jnp.int32

    def relative(block, rank):
        return (
            ((rank // shard_block) ^ my_block) * shard_rows
            + block * shard_block
            + rank % shard_block
        )

    target = inverse_order // row_count
    anchor_row = relative(target, bucket_rank(target, devices_dp))
    all_rows = jnp.arange(row_count, dtype=ints)
    pick_own = (anchor_row[None, :] == all_rows[:shard_rows, None]).astype(BF)
    sent_tokens = dot(pick_own, tokens).astype(BF).reshape(devices_dp, shard_block, width)
    sent_cotangent = dot(pick_own, cotangent).astype(BF).reshape(devices_dp, shard_block, width)
    own_tokens = exchange(sent_tokens).reshape(shard_rows, width)
    own_cotangent = exchange(sent_cotangent).reshape(shard_rows, width)
    low_tokens = gather_rel(own_tokens, TP)
    grad_low = gather_rel(own_cotangent, TP)

    source = token_order // row_count
    local_row = relative(source, bucket_rank(source, devices_dp))
    place_pick = local_row[None, :] == all_rows[:, None]
    segment_in, place_in = segment_layout(seq_lengths[0], row_count)
    segment = jnp.sum(jnp.where(place_pick, segment_in[None, :], 0), 1)
    place = jnp.sum(jnp.where(place_pick, place_in[None, :], 0), 1)
    fill = fill_order[0]
    fill_place = (fill % 2) * row_count + fill // 2
    fill_pick = (
        fill_place[:, None] == jnp.arange(2 * row_count, dtype=ints)[None, :]
    ).astype(BF)
    expert_ids = jnp.arange(experts_all, dtype=ints)
    pair_expert = jnp.concatenate([routes[:, 0], routes[:, 1]])
    member = dot(fill_pick, (pair_expert[:, None] == expert_ids[None, :]).astype(BF))
    pair_places = jnp.arange(2 * row_count, dtype=ints)
    earlier = (pair_places[None, :] < pair_places[:, None]).astype(BF)
    ranks = (member * (dot(earlier, member.astype(BF)) + 1.0)).astype(BF)
    pair_ranks = dot_t(fill_pick, ranks)
    token_ranks = (pair_ranks[:row_count] + pair_ranks[row_count:]).astype(BF)
    place_low = place_pick.astype(BF)
    row_ranks = dot(place_low, token_ranks).astype(ints)
    expert_sums = dot(
        place_low, jnp.broadcast_to((routes[:, :1] + routes[:, 1:] + 1), (row_count, 128)).astype(BF)
    ).astype(BF)
    target_expert = jnp.arange(devices_dp, dtype=ints) // copies * per_dp + pick
    target_ranks = jnp.sum(
        jnp.where(target_expert[:, None, None] == expert_ids[None, None, :], row_ranks[None], 0), 2
    )
    slots = my_part * part_rows + 1 + jnp.arange(part_rows, dtype=ints)
    slot_pick = (
        (target_ranks[:, None, :] == slots[None, :, None])
        .astype(BF)
        .reshape(devices_dp * part_rows, row_count)
    )

    grad_wide = jnp.concatenate([grad_low, expert_sums], 1)
    sent_grads = dot(slot_pick, grad_wide).astype(BF)
    got_grads = exchange(sent_grads.reshape(devices_dp, part_rows, -1))
    got_grads = gather_rel(got_grads.reshape(devices_dp * part_rows, -1), sub_axes)

    balanced = low_tokens.astype(F32)
    root_attn = inverse_root(balanced)
    normed_attn_low = (balanced * root_attn * gain_attn).astype(BF)
    cosine, sine = rope_tables(place, HD)
    cosine = cosine[:, None, :]
    sine = sine[:, None, :]
    projected = dot(normed_attn_low, w_qkv).reshape(row_count, heads, 3, HD)
    query = rope_turn(projected[:, :, 0], cosine, sine).astype(BF)
    keys = rope_turn(projected[:, :, 1], cosine, sine).astype(BF)
    values = projected[:, :, 2].astype(BF)
    allowed = ((segment[:, None] == segment[None, :]) & (place[None, :] <= place[:, None]))[None]
    scale = HD**-0.5

    def score():
        scores = jnp.einsum("qhd,khd->hqk", query, keys, preferred_element_type=F32) * scale
        return jnp.where(allowed, scores, -1e30)

    scores = score()
    top_score = jnp.max(scores, -1, keepdims=True)
    exponent_vals = jnp.exp(scores - top_score)
    row_total = jnp.sum(exponent_vals, -1, keepdims=True)
    weights = exponent_vals / row_total
    mixed = jnp.einsum("hqk,khd->qhd", weights.astype(BF), values, preferred_element_type=F32)
    mixed_low = mixed.reshape(row_count, heads * HD).astype(BF)
    attn_part = dot(mixed_low, w_out)

    def half_sum(part):
        half = part[:half_rows] + swap(part[half_rows:].astype(BF), "lo").astype(F32)
        half = half.astype(BF)
        got = swap(jnp.concatenate([half[shard_rows:], half[:shard_rows]], 0), "hi")
        return half.astype(F32) + got.astype(F32)

    def own_sum(part):
        half = part[:half_rows] + swap(part[half_rows:].astype(BF), "lo").astype(F32)
        return half[:shard_rows] + swap(half[shard_rows:].astype(BF), "hi").astype(F32)

    after_attn = balanced[:half_rows] + half_sum(attn_part)
    root_ffn = inverse_root(after_attn)
    normed_low = gather_rel((after_attn * root_ffn * gain_ffn).astype(BF), ("lo",))

    sent_rows = dot(slot_pick, normed_low).astype(BF).reshape(devices_dp, part_rows, width)
    got_rows = exchange(sent_rows).reshape(devices_dp * part_rows, width)
    rows = gather_rel(got_rows, sub_axes)

    shared_gate = dot(normed_low, w_shared_gate)
    shared_up = dot(normed_low, w_shared_up)
    shared_act, shared_slope = silu_parts(shared_gate)
    shared_hidden = (shared_act * shared_up).astype(BF)
    shared_part = dot(shared_hidden, w_shared_down)
    shared_hidden_grad = dot_bt(grad_low, w_shared_down)
    grad_sgate = (shared_hidden_grad * shared_up * shared_slope).astype(BF)
    grad_sup = (shared_hidden_grad * shared_act).astype(BF)
    shared_normed_grad = dot_bt(grad_sgate, w_shared_gate) + dot_bt(grad_sup, w_shared_up)
    shared_grads = jnp.concatenate(
        [
            dot_t(normed_low, grad_sgate),
            dot_t(normed_low, grad_sup),
            dot_t(grad_low, shared_hidden),
        ],
        1,
    )

    grad_rows = got_grads[:, :width]
    other = got_grads[:, width : width + 1].astype(ints) - 1 - my_expert
    valid = got_grads[:, width : width + 1] > 0
    part_of = jnp.arange(sub, dtype=ints) ^ my_part
    order_key = (
        jnp.arange(devices_dp, dtype=ints)[None, :, None] * slot_rows
        + part_of[:, None, None] * part_rows
        + jnp.arange(part_rows, dtype=ints)[None, None, :]
    ).reshape(-1)
    before = (order_key[None, :] < order_key[:, None]).astype(BF)
    filled = dot(before, jnp.broadcast_to(valid, (valid.shape[0], 128)).astype(BF))[:, :1]
    kept = valid & (filled < capacity)
    logits = dot(rows, w_router)
    is_mine = (expert_ids == my_expert)[None, :]
    is_other = expert_ids[None, :] == other
    gap = jnp.sum(jnp.where(is_mine, logits, 0.0) - jnp.where(is_other, logits, 0.0), 1, keepdims=True)
    gate = jax.nn.sigmoid(gap)
    gate_other = jax.nn.sigmoid(-gap)
    expert_gate = dot(rows, routed_gate_weight)
    expert_up = dot(rows, routed_up_weight)
    expert_act, expert_slope = silu_parts(expert_gate)
    expert_hidden = (expert_act * expert_up).astype(BF)
    expert_part = dot(expert_hidden, w_expert_down).astype(BF)
    expert_part = jnp.where(kept, expert_part, jnp.zeros((), BF))
    pair_grads = jnp.where(kept, gate * grad_rows.astype(F32), 0.0).astype(BF)
    gate_grad = jnp.sum(expert_part.astype(F32) * grad_rows.astype(F32), 1, keepdims=True)
    chosen_grad = gate * gate_other * gate_grad
    logit_grad = (chosen_grad * (is_mine.astype(F32) - is_other.astype(F32))).astype(BF)
    hidden_grad = dot_bt(pair_grads, w_expert_down)
    grad_egate = (hidden_grad * expert_up * expert_slope).astype(BF)
    grad_eup = (hidden_grad * expert_act).astype(BF)
    row_grads = (dot_bt(grad_egate, routed_gate_weight) + dot_bt(grad_eup, routed_up_weight)).astype(
        BF
    ).astype(F32) + dot_bt(logit_grad, w_router)

    def sub_sum(part):
        for axis in reversed(sub_axes):
            half = part.shape[0] // 2
            part = part[:half].astype(F32) + swap(part[half:].astype(BF), axis).astype(F32)
        return part

    own_slots = devices_dp * part_rows
    back_grads = sub_sum(row_grads).astype(BF).reshape(devices_dp, part_rows, width)
    back_grads = exchange(back_grads).reshape(own_slots, width)
    back_parts = (gate[:own_slots] * sub_sum(expert_part)).astype(BF)
    back_parts = exchange(back_parts.reshape(devices_dp, part_rows, width)).reshape(
        own_slots, width
    )
    grad_w_expert_down = dot_t(expert_hidden, pair_grads)
    grad_w_expert_gate = dot_t(rows, grad_egate)
    grad_w_expert_up = dot_t(rows, grad_eup)
    router_part = dot_t(logit_grad, rows)

    normed_grad = half_sum(shared_normed_grad + dot_t(slot_pick, back_grads))
    grad_out = grad_low[:half_rows].astype(F32)
    after_grad = grad_out + rms_backward(after_attn, root_ffn, gain_ffn, normed_grad)
    after_grad_low = gather_rel(after_grad.astype(BF), ("lo",))
    gain_ffn_part = 0.5 * jnp.sum(normed_grad * after_attn * root_ffn, 0)

    ffn_total = own_sum(shared_part + dot_t(slot_pick, back_parts))
    result = (after_attn[:shard_rows] + ffn_total).astype(BF)

    grad_w_out = dot_t(after_grad_low, mixed_low)
    mixed_grad = dot_bt(after_grad_low, w_out).astype(BF).reshape(row_count, heads, HD)
    weight_grad = jnp.einsum("qhd,khd->hqk", mixed_grad, values, preferred_element_type=F32)
    row_delta = jnp.sum(weights * weight_grad, -1, keepdims=True)
    grad_scores = (weights * (weight_grad - row_delta)).astype(BF)
    query_grad = jnp.einsum("hqk,khd->qhd", grad_scores, keys, preferred_element_type=F32) * scale
    key_grad = jnp.einsum("hqk,qhd->khd", grad_scores, query, preferred_element_type=F32) * scale
    value_grad = jnp.einsum(
        "hqk,qhd->khd", weights.astype(BF), mixed_grad, preferred_element_type=F32
    )
    projected_grad = jnp.stack(
        [rope_back(query_grad, cosine, sine), rope_back(key_grad, cosine, sine), value_grad], 2
    )
    projected_grad = projected_grad.astype(BF).reshape(row_count, heads * 3 * HD)
    attn_grad_part = dot_bt(projected_grad, w_qkv)
    gain_attn_part = jnp.sum(attn_grad_part * balanced * root_attn, 0)
    attn_normed_grad = own_sum(attn_grad_part)
    input_grad = after_grad[:shard_rows] + rms_backward(
        balanced[:shard_rows], root_attn[:shard_rows], gain_attn, attn_normed_grad
    )
    grad_w_qkv = dot_t(normed_attn_low, projected_grad)

    def to_initial(own):
        got = exchange(own.reshape(devices_dp, shard_block, width)).reshape(shard_rows, width)
        got = gather_rel(got, TP)
        back_pick = (anchor_row[:, None] == all_rows[None, :]).astype(BF)
        return dot(back_pick, got).astype(BF)

    final = to_initial(result)
    grad_tokens = to_initial(input_grad.astype(BF))

    small = jnp.concatenate(
        [gain_ffn_part[None], gain_attn_part[None], router_part, jnp.zeros((6, width), F32)], 0
    )
    small = small + swap(small, "hi")
    small = small + swap(small, "lo")
    small = small.reshape(-1, devices_dp, width // devices_dp).transpose(1, 0, 2)
    small = jnp.sum(exchange(small), 0)
    grad_shared = scatter_dp(shared_grads)
    hidden = w_shared_gate.shape[1]
    return (
        final,
        grad_tokens,
        small[1],
        scatter_dp(grad_w_qkv),
        scatter_dp(grad_w_out).T,
        small[0],
        small[2 : 2 + experts_all].T,
        grad_shared[:, :hidden],
        grad_shared[:, hidden : 2 * hidden],
        grad_shared[:, 2 * hidden :].T,
        grad_w_expert_gate,
        grad_w_expert_up,
        grad_w_expert_down,
    )


def solution(mesh):
    devices_dp, devices_tp = mesh.shape["dp"], mesh.shape["tensor"]
    fine = Mesh(
        mesh.devices.reshape(devices_dp // 2, 2, devices_tp // 2, 2), ("dz", "dy", "hi", "lo")
    )
    every = DP + TP
    return jax.shard_map(
        on_device,
        mesh=fine,
        in_specs=(
            P(DP, None),
            P(DP, None),
            P(),
            P(None, TP),
            P(TP, None),
            P(),
            P(),
            P(None, TP),
            P(None, TP),
            P(TP, None),
            P(None, every),
            P(None, every),
            P(every, None),
            P(DP, None),
            P(DP),
            P(DP),
            P(DP, None),
            P(DP, None),
        ),
        out_specs=(
            P(DP, None),
            P(DP, None),
            P(DP),
            P(DP, TP),
            P(TP, DP),
            P(DP),
            P(DP, None),
            P(DP, TP),
            P(DP, TP),
            P(TP, DP),
            P(None, every),
            P(None, every),
            P(every, None),
        ),
        check_vma=False,
    )
```

time: 955 us -> 361 us (0.38)
  waiting for transfers between devices: 591 us -> 102 us
  local copies, waits for them, and re-layouts: 125 us -> 36.9 us
  starting transfers between devices: 47.7 us -> 79.3 us
  blocking collectives: 25.6 us -> 0 us
  other arithmetic: 60 us -> 38.3 us
  matrix products: 78.2 us -> 98.1 us
  between operations: 16.5 us -> 2.75 us
    reduce_scatter x4 -> x0, waiting for transfers between devices: 267 us -> none  [the longest x1 69.7 us: on_device(): lax.psum_scatter(grad_w_qkv, 'dp', scatter_dimension=0, tiled=True)]
    psum x4 -> x0, waiting for transfers between devices: 101 us -> none  [the longest x1 34 us: on_device(): lax.psum(ffn_part.astype(jnp.bfloat16), 'tensor').astype(jnp.float32)]
    all_to_all x9, waiting for transfers between devices: 137 us -> 47.6 us  [exchange(): return lax.all_to_all(values, DP, split_axis=0, concat_axis=0, tiled=True)]
    unnamed x12 -> x0, waiting for transfers between devices: 86.1 us -> none
    gather x18 -> x0, local copies, waits for them, and re-layouts: 71.8 us -> none  [the longest x2 14.4 us: pair_collect(): returned[(first_target + replica) * slot_rows + rank_of].astype(jnp.float32)]
    ppermute x0 -> x33, waiting for transfers between devices: none -> 54.6 us  [the longest x27 49 us: swap(): return lax.ppermute(values, axis, [(0, 1), (1, 0)])]
    ppermute x0 -> x33, starting transfers between devices: none -> 26 us  [the longest x27 17.6 us: swap(): return lax.ppermute(values, axis, [(0, 1), (1, 0)])]
    reduce_sum x9 -> x7, other arithmetic: 25.1 us -> 3.34 us  [the longest x2 1.45 us: inverse_root(): return lax.rsqrt(jnp.mean(values * values, -1, keepdims=True) + EPSILON)]
  transfers between devices with their start and end apart: 19 -> 42, of which waited for: 16 -> 21; matrix products, arithmetic and copies ran while one was open for 19% -> 45% of each run, Pallas kernels for 0% -> 0%
where the time goes in v1:
time: 361 us; the launch traced here: 358 us
  waiting for transfers between devices  102 us (28%)
  matrix products  98.1 us (27%)
  starting transfers between devices  79.3 us (22%)
  other arithmetic  38.3 us (11%)
  local copies, waits for them, and re-layouts  36.9 us (10%)
    all_to_all x9, starting transfers between devices, exchange(): return lax.all_to_all(values, DP, split_axis=0, concat_axis=0, tiled=True)  53.3 us
    ppermute x27, waiting for transfers between devices, swap(): return lax.ppermute(values, axis, [(0, 1), (1, 0)])  49 us
    all_to_all x9, waiting for transfers between devices, exchange(): return lax.all_to_all(values, DP, split_axis=0, concat_axis=0, tiled=True)  47.6 us
    dot_general x21, matrix products, dot(): return jnp.dot(left, right, preferred_element_type=F32)  38.5 us
    dot_general x12, matrix products, dot_t(): lax.dot_general(left, right, (((0,), (0,)), ((), ())), preferred_element_...  29.1 us
    dot_general x9, matrix products, dot_bt(): lax.dot_general(left, right, (((1,), (1,)), ((), ())), preferred_element_...  18.7 us
    ppermute x27, starting transfers between devices, swap(): return lax.ppermute(values, axis, [(0, 1), (1, 0)])  17.6 us
    unnamed x211, local copies, waits for them, and re-layouts  9.04 us
  transfers between devices with their start and end apart: 42, of which 21 were waited for; matrix products, arithmetic and copies ran while one was open for 45% of the time, Pallas kernels for 0%

profile of v1, /device:TPU:0, one launch (start us, length us, event | category | flops | bytes accessed | tf_op | source)
XLA Modules:
  0.0 357.5 jit_solution(1714238901606397876)
XLA Ops:
  1.8 2.1 convolution_convert_fusion.7
  4.0 7.3 %all-to-all-start = ((bf16[8,16,768]{2,1,0:T(8,128)(2,1)}), bf16[8,16,768]{2,1,0:T(8,128)(2,1)S(1)}, u32[]{:S(2)}, u32[]{:S(2)}) async-start(bf16[8,16,768]{2,1,0:T(8,128)(2,1)} %bitcast), calls=%async_computation | async-start | bytes 393216 | tf_op jit(solution)/shard_map/all_to_all | solution.py:37
  16.0 3.2 all-to-all-done
  19.2 3.4 all-to-all-start.2
  24.5 3.9 %collective-permute-done = bf16[128,768]{1,0:T(8,128)(2,1)S(1)} collective-permute-done((bf16[128,768]{1,0:T(8,128)(2,1)S(1)}, bf16[128,768]{1,0:T(8,128)(2,1)S(1)}, u32[]{:S(2)}, u32[]{:S(2)}) %collective-permute-start) | collective-permute-done | bytes 196640 | tf_op jit(solution)/shard_map/ppermute | solution.py:27
  30.9 1.9 fusion.89
  34.0 4.1 %fusion.176 = (f32[3,512]{1,0:T(4,128)S(1)}, f32[3,512,512]{1,2,0:T(8,128)}) fusion(pred[512,512]{0,1:T(8,128)(4,1)} %compare_and_fusion, bf16[512,3,32]{0,2,1:T(8,128)(2,1)S(1)} %get-tuple-element.52, bf16[512,3,32]{0,2,1:T(8,128)(2,1)S(1)} %get-tuple-element.53, bf16[512,3,32]{0,2,1:T(8,128)(2,1)S(1)} %get-tuple-element.43, ...), kind=kOutput, calls=%fused_computation.355 | convolution fusion | flops 104595968 | bytes 3807232 | tf_op jit(solution)/shard_map/sub | solution.py:239
  38.2 2.5 convolution_convert_fusion.6
  49.2 2.5 collective-permute-done.6
  52.7 7.1 %collective-permute-done.3 = bf16[256,768]{1,0:T(8,128)(2,1)} collective-permute-done((bf16[256,768]{1,0:T(8,128)(2,1)}, bf16[256,768]{1,0:T(8,128)(2,1)}, u32[]{:S(2)}, u32[]{:S(2)}) %collective-permute-start.3) | collective-permute-done | bytes 393248 | tf_op jit(solution)/shard_map/ppermute | solution.py:27
  63.4 2.6 convolution_convert_fusion.1
  66.0 17.9 %all-to-all-start.3 = ((bf16[8,64,896]{2,1,0:T(8,128)(2,1)}), bf16[8,64,896]{2,1,0:T(8,128)(2,1)S(1)}, u32[]{:S(2)}, u32[]{:S(2)}) async-start(bf16[8,64,896]{2,1,0:T(8,128)(2,1)} %bitcast.201), calls=%async_computation.3 | async-start | bytes 1835008 | tf_op jit(solution)/shard_map/all_to_all | solution.py:37
  83.9 2.0 fusion.164
  86.0 1.8 fusion.163
  87.8 1.9 multiply_convert_fusion.6
  89.8 1.9 fusion.85
  91.7 1.7 fusion.161
  93.5 1.7 fusion.162
  95.2 2.5 pad_maximum_fusion
  97.7 6.1 %copy.106 = f32[768,1536]{1,0:T(8,128)} copy(f32[768,1536]{0,1:T(8,128)} %pad_maximum_fusion) | data formatting | bytes 9437184 | tf_op jit(solution)/shard_map/concatenate | solution.py:273
  103.8 2.6 convolution_convert_fusion.4
  107.4 5.1 %all-to-all-start.1 = ((bf16[8,64,768]{2,1,0:T(8,128)(2,1)}), bf16[8,64,768]{2,1,0:T(8,128)(2,1)}, u32[]{:S(2)}, u32[]{:S(2)}) async-start(bf16[8,64,768]{2,1,0:T(8,128)(2,1)} %bitcast.202), calls=%async_computation.1 | async-start | bytes 1572864 | tf_op jit(solution)/shard_map/all_to_all | solution.py:37
  112.5 2.8 fusion.27
  115.3 2.0 collective-permute-start.30
  118.7 3.1 fusion.178
  123.1 3.1 fusion.179
  126.1 6.7 %all-to-all-done.1 = bf16[8,64,768]{2,1,0:T(8,128)(2,1)} async-done(((bf16[8,64,768]{2,1,0:T(8,128)(2,1)}), bf16[8,64,768]{2,1,0:T(8,128)(2,1)}, u32[]{:S(2)}, u32[]{:S(2)}) %all-to-all-start.1) | async-done | bytes 786464 | tf_op jit(solution)/shard_map/all_to_all | solution.py:37
  132.8 16.2 %collective-permute-done.30 = bf16[4,96,1536]{2,1,0:T(8,128)(2,1)} collective-permute-done((bf16[4,96,1536]{2,1,0:T(8,128)(2,1)}, bf16[4,96,1536]{2,1,0:T(8,128)(2,1)}, u32[]{:S(2)}, u32[]{:S(2)}) %collective-permute-start.30) | collective-permute-done | bytes 1179680 | tf_op jit(solution)/shard_map/ppermute | solution.py:27
  149.0 2.3 bitcast_add_fusion
  155.6 2.0 subtract_reduce_fusion
  157.7 3.0 fusion.169
  160.7 2.9 fusion.168
  163.7 4.8 %multiply_convert_fusion = (bf16[1024,1024]{1,0:T(8,128)(2,1)S(1)}, bf16[1024,1024]{1,0:T(8,128)(2,1)S(1)}, bf16[1024,1024]{1,0:T(8,128)(2,1)S(1)}) fusion(f32[1024,1024]{1,0:T(8,128)S(1)} %fusion.169, f32[1024,1024]{1,0:T(8,128)S(1)} %fusion.168, bf16[1024,768]{1,0:T(8,128)(2,1)S(1)} %copy-done, f32[1024]{0:T(1024)S(1)} %add_divide_fusion.2, ...), kind=kOutput, calls=%fused_computation.2 | convolution fusion | flops 1631846400 | bytes 18093056 | tf_op jit(solution)/shard_map/dot_general | solution.py:23
  168.5 3.8 %fusion.9 = (f32[1024]{0:T(1024)S(1)}, bf16[1024,768]{0,1:T(8,128)(2,1)S(1)}) fusion(bf16[512,896]{0,1:T(8,128)(2,1)} %collective-permute-done.8, bf16[512,896]{0,1:T(8,128)(2,1)S(1)} %copy-done.9, bf16[1024,1024]{1,0:T(8,128)(2,1)S(1)} %get-tuple-element.27, bf16[1024,768]{1,0:T(8,128)(2,1)S(1)} %copy-done, pred[1024]{0:T(1024)(128)(4,1)S(1)} %fusion.39), kind=kOutput, calls=%fused_computation.18 | convolution fusion | flops 1617689600 | bytes 7083008 | tf_op jit(solution)/shard_map/dot_general | solution.py:15
  172.5 1.8 fusion.181
  174.3 3.4 add_convert_fusion
  179.2 4.4 %all-to-all-start.4 = ((bf16[8,64,768]{2,1,0:T(8,128)(2,1)}), bf16[8,64,768]{2,1,0:T(8,128)(2,1)}, u32[]{:S(2)}, u32[]{:S(2)}) async-start(bf16[8,64,768]{2,1,0:T(8,128)(2,1)} %bitcast.21), calls=%async_computation.4 | async-start | bytes 1572864 | tf_op jit(solution)/shard_map/all_to_all | solution.py:37
  185.6 1.8 fusion.180
  188.6 2.9 collective-permute-start.32
  192.6 18.8 %all-to-all-done.4 = bf16[8,64,768]{2,1,0:T(8,128)(2,1)} async-done(((bf16[8,64,768]{2,1,0:T(8,128)(2,1)}), bf16[8,64,768]{2,1,0:T(8,128)(2,1)}, u32[]{:S(2)}, u32[]{:S(2)}) %all-to-all-start.4) | async-done | bytes 786464 | tf_op jit(solution)/shard_map/all_to_all | solution.py:37
  211.4 4.2 %all-to-all-start.6 = ((bf16[8,64,768]{2,1,0:T(8,128)(2,1)}), bf16[8,64,768]{2,1,0:T(8,128)(2,1)}, u32[]{:S(2)}, u32[]{:S(2)}) async-start(bf16[8,64,768]{2,1,0:T(8,128)(2,1)} %bitcast.188), calls=%async_computation.6 | async-start | bytes 1572864 | tf_op jit(solution)/shard_map/all_to_all | solution.py:37
  219.2 4.8 %fusion.23 = f32[1024,768]{1,0:T(8,128)} fusion(bf16[1024,1024]{1,0:T(8,128)(2,1)S(1)} %copy-done.103, f32[1024]{0:T(1024)S(1)} %copy-done.75, pred[1024]{0:T(1024)(128)(4,1)S(1)} %fusion.39, bf16[512,896]{0,1:T(8,128)(2,1)} %collective-permute-done.8, bf16[512,896]{0,1:T(8,128)(2,1)S(1)} %copy-done.9), kind=kOutput, calls=%fused_computation.60 | convolution fusion | flops 1616117760 | bytes 7083008 | tf_op jit(solution)/shard_map/dot_general | solution.py:19
  223.9 1.9 bitcast_add_fusion.2
  227.3 8.4 %all-to-all-done.6 = bf16[8,64,768]{2,1,0:T(8,128)(2,1)} async-done(((bf16[8,64,768]{2,1,0:T(8,128)(2,1)}), bf16[8,64,768]{2,1,0:T(8,128)(2,1)}, u32[]{:S(2)}, u32[]{:S(2)}) %all-to-all-start.6) | async-done | bytes 786464 | tf_op jit(solution)/shard_map/all_to_all | solution.py:37
  235.6 2.5 bitcast_add_fusion.1
  238.3 4.8 %fusion.167 = f32[768,1024]{1,0:T(8,128)} fusion(bf16[1024,1024]{1,0:T(8,128)(2,1)S(1)} %copy-done.101, bf16[512,768]{1,0:T(8,128)(2,1)S(1)} %copy-done.93, bf16[512,768]{1,0:T(8,128)(2,1)} %bitcast.15), kind=kOutput, calls=%fused_computation.346 | convolution fusion | flops 1613758464 | bytes 6815744 | tf_op jit(solution)/shard_map/dot_general | solution.py:19
  245.5 4.7 %fusion.166 = f32[768,1024]{1,0:T(8,128)} fusion(bf16[1024,1024]{1,0:T(8,128)(2,1)S(1)} %copy-done.99, bf16[512,768]{1,0:T(8,128)(2,1)S(1)} %copy-done.93, bf16[512,768]{1,0:T(8,128)(2,1)} %bitcast.15), kind=kOutput, calls=%fused_computation.345 | convolution fusion | flops 1613758464 | bytes 6815744 | tf_op jit(solution)/shard_map/dot_general | solution.py:19
  251.7 3.7 %all-to-all-start.5 = ((bf16[8,16,768]{2,1,0:T(8,128)(2,1)}), bf16[8,16,768]{2,1,0:T(8,128)(2,1)S(1)}, u32[]{:S(2)}, u32[]{:S(2)}) async-start(bf16[8,16,768]{2,1,0:T(8,128)(2,1)} %bitcast.23), calls=%async_computation.5 | async-start | bytes 393216 | tf_op jit(solution)/shard_map/all_to_all | solution.py:37
  255.4 3.5 collective-permute-done.16
  259.3 1.9 fusion.171
  261.2 2.2 fusion.101
  265.0 5.7 %collective-permute-done.12 = bf16[128,768]{1,0:T(8,128)(2,1)S(1)} collective-permute-done((bf16[128,768]{1,0:T(8,128)(2,1)S(1)}, bf16[128,768]{1,0:T(8,128)(2,1)S(1)}, u32[]{:S(2)}, u32[]{:S(2)}) %collective-permute-start.12) | collective-permute-done | bytes 196640 | tf_op jit(solution)/shard_map/ppermute | solution.py:27
  272.0 2.6 convolution_bitcast_fusion
  292.9 3.1 collective-permute-done.27
  300.9 1.7 copy.104
  313.6 4.0 %all-to-all-start.8 = ((f32[8,24,96]{2,1,0:T(8,128)}), f32[8,24,96]{2,1,0:T(8,128)}, u32[]{:S(2)}, u32[]{:S(2)}) async-start(f32[8,24,96]{2,1,0:T(8,128)} %bitcast.214), calls=%async_computation.8 | async-start | bytes 196608 | tf_op jit(solution)/shard_map/all_to_all | solution.py:37
  319.2 5.6 %all-to-all-done.8 = f32[8,24,96]{2,1,0:T(8,128)} async-done(((f32[8,24,96]{2,1,0:T(8,128)}), f32[8,24,96]{2,1,0:T(8,128)}, u32[]{:S(2)}, u32[]{:S(2)}) %all-to-all-start.8) | async-done | bytes 73760 | tf_op jit(solution)/shard_map/all_to_all | solution.py:37
  328.1 4.5 %collective-permute-done.19 = bf16[128,768]{1,0:T(8,128)(2,1)S(1)} collective-permute-done((bf16[128,768]{1,0:T(8,128)(2,1)S(1)}, bf16[128,768]{1,0:T(8,128)(2,1)S(1)}, u32[]{:S(2)}, u32[]{:S(2)}) %collective-permute-start.19) | collective-permute-done | bytes 196640 | tf_op jit(solution)/shard_map/ppermute | solution.py:27
  333.7 3.4 all-to-all-start.7
  338.3 2.0 collective-permute-start.25
  340.8 4.0 %all-to-all-done.7 = bf16[8,16,768]{2,1,0:T(8,128)(2,1)S(1)} async-done(((bf16[8,16,768]{2,1,0:T(8,128)(2,1)}), bf16[8,16,768]{2,1,0:T(8,128)(2,1)S(1)}, u32[]{:S(2)}, u32[]{:S(2)}) %all-to-all-start.7) | async-done | bytes 196640 | tf_op jit(solution)/shard_map/all_to_all | solution.py:37
  347.0 1.8 collective-permute-start.26
  350.6 2.5 convolution_convert_fusion.3
  354.9 2.4 convolution_convert_fusion.2
  (404 shorter events, 97.0 us)
Async XLA Ops:
  0.6 163.0 %copy-start = (bf16[1024,768]{1,0:T(8,128)(2,1)S(1)}, bf16[1024,768]{1,0:T(8,128)(2,1)}, u32[]{:S(2)}) copy-start(bf16[1024,768]{1,0:T(8,128)(2,1)} %param.30) | copy-start | bytes 4718596
  0.7 10.6 %copy-start.95 = (s32[1,8]{1,0:T(1,128)S(1)}, s32[1,8]{1,0:T(1,128)}, u32[]{:S(2)}) copy-start(s32[1,8]{1,0:T(1,128)} %param.31) | copy-start | bytes 100
  0.7 11.6 %copy-start.73 = (s32[512,2]{0,1:T(2,128)S(1)}, s32[512,2]{0,1:T(2,128)}, u32[]{:S(2)}) copy-start(s32[512,2]{0,1:T(2,128)} %param.34) | copy-start | bytes 12292
  0.7 11.6 %copy-start.84 = (s32[1,1024]{1,0:T(1,128)S(1)}, s32[1,1024]{1,0:T(1,128)}, u32[]{:S(2)}) copy-start(s32[1,1024]{1,0:T(1,128)} %param.35) | copy-start | bytes 12292
  1.8 13.1 %copy-start.67 = (s32[512]{0:T(512)}, s32[512]{0:T(512)S(1)}, u32[]{:S(2)}) copy-start(s32[512]{0:T(512)S(1)} %fusion.127) | copy-start | bytes 6148
  4.0 15.2 %all-to-all-start = ((bf16[8,16,768]{2,1,0:T(8,128)(2,1)}), bf16[8,16,768]{2,1,0:T(8,128)(2,1)S(1)}, u32[]{:S(2)}, u32[]{:S(2)}) async-start(bf16[8,16,768]{2,1,0:T(8,128)(2,1)} %bitcast), calls=%async_computation | async-start | bytes 393216 | tf_op jit(solution)/shard_map/all_to_all | solution.py:37
  11.8 32.2 %copy-start.76 = (s32[512]{0:T(512)}, s32[512]{0:T(512)S(1)}, u32[]{:S(2)}) copy-start(s32[512]{0:T(512)S(1)} %fusion.132) | copy-start | bytes 6148
  15.0 15.9 %copy-start.65 = (f32[768]{0:T(1024)S(1)}, f32[768]{0:T(1024)}, u32[]{:S(2)}) copy-start(f32[768]{0:T(1024)} %param.20) | copy-start | bytes 9220
  19.2 25.2 %all-to-all-start.2 = ((bf16[8,16,768]{2,1,0:T(8,128)(2,1)}), bf16[8,16,768]{2,1,0:T(8,128)(2,1)S(1)}, u32[]{:S(2)}, u32[]{:S(2)}) async-start(bf16[8,16,768]{2,1,0:T(8,128)(2,1)} %bitcast.16), calls=%async_computation.2 | async-start | bytes 393216 | tf_op jit(solution)/shard_map/all_to_all | solution.py:37
  22.6 5.8 %collective-permute-start = (bf16[128,768]{1,0:T(8,128)(2,1)S(1)}, bf16[128,768]{1,0:T(8,128)(2,1)S(1)}, u32[]{:S(2)}, u32[]{:S(2)}) collective-permute-start(bf16[128,768]{1,0:T(8,128)(2,1)S(1)} %bitcast.180), channel_id=1, source_target_pairs={{0,2},{2,0},{1,3},{3,1},{4,6},{6,4},{5,7},{7,5},{8,10},{10,8},{9,1... | collective-permute-start | bytes 589832 | tf_op jit(solution)/shard_map/ppermute | solution.py:27
  24.5 9.4 %copy-start.42 = (f32[512,32]{0,1:T(8,128)}, f32[512,32]{0,1:T(8,128)S(1)}, u32[]{:S(2)}) copy-start(f32[512,32]{0,1:T(8,128)S(1)} %get-tuple-element.58) | copy-start | bytes 196612
  24.5 9.4 %copy-start.44 = (f32[512,32]{0,1:T(8,128)}, f32[512,32]{0,1:T(8,128)S(1)}, u32[]{:S(2)}) copy-start(f32[512,32]{0,1:T(8,128)S(1)} %get-tuple-element.59) | copy-start | bytes 196612
  28.4 24.1 %copy-start.13 = (bf16[128,768]{1,0:T(8,128)(2,1)}, bf16[128,768]{1,0:T(8,128)(2,1)S(1)}, u32[]{:S(2)}) copy-start(bf16[128,768]{1,0:T(8,128)(2,1)S(1)} %collective-permute-done) | copy-start | bytes 589828
  28.4 2.2 collective-permute-start.1
  30.7 21.9 %copy-start.10 = (bf16[256,768]{1,0:T(8,128)(2,1)}, bf16[256,768]{1,0:T(8,128)(2,1)S(1)}, u32[]{:S(2)}) copy-start(bf16[256,768]{1,0:T(8,128)(2,1)S(1)} %collective-permute-done.1) | copy-start | bytes 1179652
  43.4 2.5 collective-permute-start.2
  44.4 19.0 %copy-start.18 = (bf16[8,16,768]{2,1,0:T(8,128)(2,1)}, bf16[8,16,768]{2,1,0:T(8,128)(2,1)S(1)}, u32[]{:S(2)}) copy-start(bf16[8,16,768]{2,1,0:T(8,128)(2,1)S(1)} %all-to-all-done.2) | copy-start | bytes 589828
  44.4 7.3 %collective-permute-start.6 = (bf16[128,768]{1,0:T(8,128)(2,1)S(1)}, bf16[128,768]{1,0:T(8,128)(2,1)S(1)}, u32[]{:S(2)}, u32[]{:S(2)}) collective-permute-start(bf16[128,768]{1,0:T(8,128)(2,1)S(1)} %bitcast.191), channel_id=1, source_target_pairs={{0,2},{2,0},{1,3},{3,1},{4,6},{6,4},{5,7},{7,5},{8,10},{10,8},{9,1... | collective-permute-start | bytes 589832 | tf_op jit(solution)/shard_map/ppermute | solution.py:27
  48.1 11.7 %collective-permute-start.3 = (bf16[256,768]{1,0:T(8,128)(2,1)}, bf16[256,768]{1,0:T(8,128)(2,1)}, u32[]{:S(2)}, u32[]{:S(2)}) collective-permute-start(bf16[256,768]{1,0:T(8,128)(2,1)} %pad_maximum_fusion.9), channel_id=1, source_target_pairs={{0,2},{2,0},{1,3},{3,1},{4,6},{6,4},{5,7},{7,5},{8,10},{10,8},{9,1... | collective-permute-start | bytes 1179656 | tf_op jit(solution)/shard_map/ppermute | solution.py:27
  51.7 11.6 %copy-start.30 = (bf16[128,768]{1,0:T(8,128)(2,1)}, bf16[128,768]{1,0:T(8,128)(2,1)S(1)}, u32[]{:S(2)}) copy-start(bf16[128,768]{1,0:T(8,128)(2,1)S(1)} %collective-permute-done.6) | copy-start | bytes 589828
  52.5 10.8 %collective-permute-start.7 = (bf16[256,768]{1,0:T(8,128)(2,1)}, bf16[256,768]{1,0:T(8,128)(2,1)}, u32[]{:S(2)}, u32[]{:S(2)}) collective-permute-start(bf16[256,768]{1,0:T(8,128)(2,1)} %pad_maximum_fusion.10), channel_id=1, source_target_pairs={{0,1},{1,0},{2,3},{3,2},{4,5},{5,4},{6,7},{7,6},{8,9},{9,8},{10,11... | collective-permute-start | bytes 1179656 | tf_op jit(solution)/shard_map/ppermute | solution.py:27
  52.7 9.9 %copy-start.4 = (f32[512,768]{1,0:T(8,128)}, f32[512,768]{1,0:T(8,128)S(1)}, u32[]{:S(2)}) copy-start(f32[512,768]{1,0:T(8,128)S(1)} %fusion.165) | copy-start | bytes 4718596
  52.7 10.2 %copy-start.77 = (s32[512]{0:T(512)S(1)}, s32[512]{0:T(512)}, u32[]{:S(2)}) copy-start(s32[512]{0:T(512)} %copy-done.76) | copy-start | bytes 6148
  62.5 21.4 %collective-permute-start.4 = (bf16[256,768]{1,0:T(8,128)(2,1)}, bf16[256,768]{1,0:T(8,128)(2,1)}, u32[]{:S(2)}, u32[]{:S(2)}) collective-permute-start(bf16[256,768]{1,0:T(8,128)(2,1)} %multiply_convert_fusion.9), channel_id=1, source_target_pairs={{0,1},{1,0},{2,3},{3,2},{4,5},{5,4},{6,7},{7,6},{8,9},{9,8},{10,11... | collective-permute-start | bytes 1179656 | tf_op jit(solution)/shard_map/ppermute | solution.py:27
  66.0 41.4 %all-to-all-start.3 = ((bf16[8,64,896]{2,1,0:T(8,128)(2,1)}), bf16[8,64,896]{2,1,0:T(8,128)(2,1)S(1)}, u32[]{:S(2)}, u32[]{:S(2)}) async-start(bf16[8,64,896]{2,1,0:T(8,128)(2,1)} %bitcast.201), calls=%async_computation.3 | async-start | bytes 1835008 | tf_op jit(solution)/shard_map/all_to_all | solution.py:37
  107.4 25.4 %all-to-all-start.1 = ((bf16[8,64,768]{2,1,0:T(8,128)(2,1)}), bf16[8,64,768]{2,1,0:T(8,128)(2,1)}, u32[]{:S(2)}, u32[]{:S(2)}) async-start(bf16[8,64,768]{2,1,0:T(8,128)(2,1)} %bitcast.202), calls=%async_computation.1 | async-start | bytes 1572864 | tf_op jit(solution)/shard_map/all_to_all | solution.py:37
  115.3 33.7 %collective-permute-start.30 = (bf16[4,96,1536]{2,1,0:T(8,128)(2,1)}, bf16[4,96,1536]{2,1,0:T(8,128)(2,1)}, u32[]{:S(2)}, u32[]{:S(2)}) collective-permute-start(bf16[4,96,1536]{2,1,0:T(8,128)(2,1)} %fusion.27), channel_id=1, source_target_pairs={{0,4},{4,0},{1,5},{5,1},{2,6},{6,2},{3,7},{7,3},{8,12},{12,8},{9,1... | collective-permute-start | bytes 3538952 | tf_op jit(solution)/shard_map/ppermute | solution.py:27
  118.2 65.4 %copy-start.88 = (f32[16]{0:T(128)}, f32[16]{0:T(128)S(1)}, u32[]{:S(2)}) copy-start(f32[16]{0:T(128)S(1)} %fusion.159) | copy-start | bytes 196
  123.1 30.7 %collective-permute-start.8 = (bf16[512,896]{0,1:T(8,128)(2,1)}, bf16[512,896]{0,1:T(8,128)(2,1)}, u32[]{:S(2)}, u32[]{:S(2)}) collective-permute-start(bf16[512,896]{0,1:T(8,128)(2,1)} %copy.93), channel_id=1, source_target_pairs={{0,1},{1,0},{2,3},{3,2},{4,5},{5,4},{6,7},{7,6},{8,9},{9,8},{10,11... | collective-permute-start | bytes 2752520 | tf_op jit(solution)/shard_map/ppermute | solution.py:27
  132.8 22.8 %collective-permute-start.5 = (bf16[512,768]{1,0:T(8,128)(2,1)}, bf16[512,768]{1,0:T(8,128)(2,1)S(1)}, u32[]{:S(2)}, u32[]{:S(2)}) collective-permute-start(bf16[512,768]{1,0:T(8,128)(2,1)} %bitcast.15), channel_id=1, source_target_pairs={{0,1},{1,0},{2,3},{3,2},{4,5},{5,4},{6,7},{7,6},{8,9},{9,8},{10,11... | collective-permute-start | bytes 2359304 | tf_op jit(solution)/shard_map/ppermute | solution.py:27
  152.3 35.1 %collective-permute-start.31 = (bf16[2,96,1536]{2,1,0:T(8,128)(2,1)}, bf16[2,96,1536]{2,1,0:T(8,128)(2,1)}, u32[]{:S(2)}, u32[]{:S(2)}) collective-permute-start(bf16[2,96,1536]{2,1,0:T(8,128)(2,1)} %fusion.65), channel_id=1, source_target_pairs={{0,8},{8,0},{16,24},{24,16},{1,9},{9,1},{17,25},{25,17},{2,10},{10... | collective-permute-start | bytes 1769480 | tf_op jit(solution)/shard_map/ppermute | solution.py:55
  172.4 5.4 %collective-permute-start.9 = (bf16[512,768]{0,1:T(8,128)(2,1)S(1)}, bf16[512,768]{0,1:T(8,128)(2,1)S(1)}, u32[]{:S(2)}, u32[]{:S(2)}) collective-permute-start(bf16[512,768]{0,1:T(8,128)(2,1)S(1)} %slice.238), channel_id=1, source_target_pairs={{0,1},{1,0},{2,3},{3,2},{4,5},{5,4},{6,7},{7,6},{8,9},{9,8},{10,11... | collective-permute-start | bytes 2359304 | tf_op jit(solution)/shard_map/ppermute | solution.py:27
  179.2 32.2 %all-to-all-start.4 = ((bf16[8,64,768]{2,1,0:T(8,128)(2,1)}), bf16[8,64,768]{2,1,0:T(8,128)(2,1)}, u32[]{:S(2)}, u32[]{:S(2)}) async-start(bf16[8,64,768]{2,1,0:T(8,128)(2,1)} %bitcast.21), calls=%async_computation.4 | async-start | bytes 1572864 | tf_op jit(solution)/shard_map/all_to_all | solution.py:37
  184.4 7.1 %collective-permute-start.14 = (bf16[512,768]{1,0:T(8,128)(2,1)S(1)}, bf16[512,768]{1,0:T(8,128)(2,1)S(1)}, u32[]{:S(2)}, u32[]{:S(2)}) collective-permute-start(bf16[512,768]{1,0:T(8,128)(2,1)S(1)} %slice.332), channel_id=1, source_target_pairs={{0,1},{1,0},{2,3},{3,2},{4,5},{5,4},{6,7},{7,6},{8,9},{9,8},{10,11... | collective-permute-start | bytes 2359304 | tf_op jit(solution)/shard_map/ppermute | solution.py:27
  188.6 28.7 %collective-permute-start.32 = (bf16[1,96,1536]{2,1,0:T(8,128)(2,1)S(1)}, bf16[1,96,1536]{2,1,0:T(8,128)(2,1)}, u32[]{:S(2)}, u32[]{:S(2)}) collective-permute-start(bf16[1,96,1536]{2,1,0:T(8,128)(2,1)S(1)} %dynamic-slice_convert_fusion.3), channel_id=1, source_target_pairs={{0,16},{8,24},{16,0},{24,8},{1,17},{9,25},{17,1},{25,9},{2,18},{10... | collective-permute-start | bytes 884744 | tf_op jit(solution)/shard_map/ppermute | solution.py:55
  211.4 24.2 %all-to-all-start.6 = ((bf16[8,64,768]{2,1,0:T(8,128)(2,1)}), bf16[8,64,768]{2,1,0:T(8,128)(2,1)}, u32[]{:S(2)}, u32[]{:S(2)}) async-start(bf16[8,64,768]{2,1,0:T(8,128)(2,1)} %bitcast.188), calls=%async_computation.6 | async-start | bytes 1572864 | tf_op jit(solution)/shard_map/all_to_all | solution.py:37
  223.9 11.7 %copy-start.23 = (f32[512,768]{1,0:T(8,128)S(1)}, f32[512,768]{1,0:T(8,128)}, u32[]{:S(2)}) copy-start(f32[512,768]{1,0:T(8,128)} %fusion.179) | copy-start | bytes 4718596
  227.2 15.9 %collective-permute-start.10 = (bf16[256,768]{1,0:T(8,128)(2,1)S(1)}, bf16[256,768]{1,0:T(8,128)(2,1)S(1)}, u32[]{:S(2)}, u32[]{:S(2)}) collective-permute-start(bf16[256,768]{1,0:T(8,128)(2,1)S(1)} %slice.335), channel_id=1, source_target_pairs={{0,1},{1,0},{2,3},{3,2},{4,5},{5,4},{6,7},{7,6},{8,9},{9,8},{10,11... | collective-permute-start | bytes 1179656 | tf_op jit(solution)/shard_map/ppermute | solution.py:27
  238.2 6.6 %collective-permute-start.15 = (bf16[256,768]{1,0:T(8,128)(2,1)S(1)}, bf16[256,768]{1,0:T(8,128)(2,1)S(1)}, u32[]{:S(2)}, u32[]{:S(2)}) collective-permute-start(bf16[256,768]{1,0:T(8,128)(2,1)S(1)} %slice.334), channel_id=1, source_target_pairs={{0,1},{1,0},{2,3},{3,2},{4,5},{5,4},{6,7},{7,6},{8,9},{9,8},{10,11... | collective-permute-start | bytes 1179656 | tf_op jit(solution)/shard_map/ppermute | solution.py:27
  243.2 7.8 %collective-permute-start.11 = (bf16[128,768]{1,0:T(8,128)(2,1)S(1)}, bf16[128,768]{1,0:T(8,128)(2,1)S(1)}, u32[]{:S(2)}, u32[]{:S(2)}) collective-permute-start(bf16[128,768]{1,0:T(8,128)(2,1)S(1)} %slice.338), channel_id=1, source_target_pairs={{0,2},{2,0},{1,3},{3,1},{4,6},{6,4},{5,7},{7,5},{8,10},{10,8},{9,1... | collective-permute-start | bytes 589832 | tf_op jit(solution)/shard_map/ppermute | solution.py:27
  244.9 13.9 %collective-permute-start.16 = (bf16[256,768]{1,0:T(8,128)(2,1)S(1)}, bf16[256,768]{1,0:T(8,128)(2,1)S(1)}, u32[]{:S(2)}, u32[]{:S(2)}) collective-permute-start(bf16[256,768]{1,0:T(8,128)(2,1)S(1)} %pad_maximum_fusion.12), channel_id=1, source_target_pairs={{0,2},{2,0},{1,3},{3,1},{4,6},{6,4},{5,7},{7,5},{8,10},{10,8},{9,1... | collective-permute-start | bytes 1179656 | tf_op jit(solution)/shard_map/ppermute | solution.py:27
  251.7 11.7 %all-to-all-start.5 = ((bf16[8,16,768]{2,1,0:T(8,128)(2,1)}), bf16[8,16,768]{2,1,0:T(8,128)(2,1)S(1)}, u32[]{:S(2)}, u32[]{:S(2)}) async-start(bf16[8,16,768]{2,1,0:T(8,128)(2,1)} %bitcast.23), calls=%async_computation.5 | async-start | bytes 393216 | tf_op jit(solution)/shard_map/all_to_all | solution.py:37
  261.2 10.3 %copy-start.58 = (bf16[192,768]{1,0:T(8,128)(2,1)S(1)}, bf16[192,768]{1,0:T(8,128)(2,1)}, u32[]{:S(2)}) copy-start(bf16[192,768]{1,0:T(8,128)(2,1)} %param.22) | copy-start | bytes 884740
  261.2 10.3 %collective-permute-start.17 = (bf16[256,768]{1,0:T(8,128)(2,1)S(1)}, bf16[256,768]{1,0:T(8,128)(2,1)S(1)}, u32[]{:S(2)}, u32[]{:S(2)}) collective-permute-start(bf16[256,768]{1,0:T(8,128)(2,1)S(1)} %get-tuple-element.19), channel_id=1, source_target_pairs={{0,1},{1,0},{2,3},{3,2},{4,5},{5,4},{6,7},{7,6},{8,9},{9,8},{10,11... | collective-permute-start | bytes 1179656 | tf_op jit(solution)/shard_map/ppermute | solution.py:27
  263.4 11.2 %copy-start.33 = (bf16[8,16,768]{2,1,0:T(8,128)(2,1)}, bf16[8,16,768]{2,1,0:T(8,128)(2,1)S(1)}, u32[]{:S(2)}) copy-start(bf16[8,16,768]{2,1,0:T(8,128)(2,1)S(1)} %all-to-all-done.5) | copy-start | bytes 589828
  263.4 7.3 %collective-permute-start.12 = (bf16[128,768]{1,0:T(8,128)(2,1)S(1)}, bf16[128,768]{1,0:T(8,128)(2,1)S(1)}, u32[]{:S(2)}, u32[]{:S(2)}) collective-permute-start(bf16[128,768]{1,0:T(8,128)(2,1)S(1)} %bitcast.203), channel_id=1, source_target_pairs={{0,2},{2,0},{1,3},{3,1},{4,6},{6,4},{5,7},{7,5},{8,10},{10,8},{9,1... | collective-permute-start | bytes 589832 | tf_op jit(solution)/shard_map/ppermute | solution.py:27
  271.5 79.1 %collective-permute-start.13 = (bf16[256,768]{1,0:T(8,128)(2,1)}, bf16[256,768]{1,0:T(8,128)(2,1)}, u32[]{:S(2)}, u32[]{:S(2)}) collective-permute-start(bf16[256,768]{1,0:T(8,128)(2,1)} %pad_maximum_fusion.11), channel_id=1, source_target_pairs={{0,1},{1,0},{2,3},{3,2},{4,5},{5,4},{6,7},{7,6},{8,9},{9,8},{10,11... | collective-permute-start | bytes 1179656 | tf_op jit(solution)/shard_map/ppermute | solution.py:27
  282.3 43.4 %collective-permute-start.18 = (bf16[256,768]{1,0:T(8,128)(2,1)}, bf16[256,768]{1,0:T(8,128)(2,1)}, u32[]{:S(2)}, u32[]{:S(2)}) collective-permute-start(bf16[256,768]{1,0:T(8,128)(2,1)} %slice.333), channel_id=1, source_target_pairs={{0,1},{1,0},{2,3},{3,2},{4,5},{5,4},{6,7},{7,6},{8,9},{9,8},{10,11... | collective-permute-start | bytes 1179656 | tf_op jit(solution)/shard_map/ppermute | solution.py:27
  284.0 7.3 %collective-permute-start.22 = (f32[24,768]{1,0:T(8,128)}, f32[24,768]{1,0:T(8,128)}, u32[]{:S(2)}, u32[]{:S(2)}) collective-permute-start(f32[24,768]{1,0:T(8,128)} %maximum_maximum_fusion), channel_id=1, source_target_pairs={{0,2},{2,0},{1,3},{3,1},{4,6},{6,4},{5,7},{7,5},{8,10},{10,8},{9,1... | collective-permute-start | bytes 221192 | tf_op jit(solution)/shard_map/ppermute | solution.py:27
  289.0 6.9 %collective-permute-start.27 = (bf16[4,96,192]{2,1,0:T(8,128)(2,1)S(1)}, bf16[4,96,192]{2,1,0:T(8,128)(2,1)S(1)}, u32[]{:S(2)}, u32[]{:S(2)}) collective-permute-start(bf16[4,96,192]{2,1,0:T(8,128)(2,1)S(1)} %fusion.90), channel_id=1, source_target_pairs={{0,4},{4,0},{1,5},{5,1},{2,6},{6,2},{3,7},{7,3},{8,12},{12,8},{9,1... | collective-permute-start | bytes 442376 | tf_op jit(solution)/shard_map/ppermute | solution.py:27
  292.9 16.0 %collective-permute-start.23 = (f32[24,768]{1,0:T(8,128)}, f32[24,768]{1,0:T(8,128)}, u32[]{:S(2)}, u32[]{:S(2)}) collective-permute-start(f32[24,768]{1,0:T(8,128)} %fusion.160), channel_id=1, source_target_pairs={{0,1},{1,0},{2,3},{3,2},{4,5},{5,4},{6,7},{7,6},{8,9},{9,8},{10,11... | collective-permute-start | bytes 221192 | tf_op jit(solution)/shard_map/ppermute | solution.py:27
  299.0 4.9 %collective-permute-start.28 = (bf16[2,96,192]{1,2,0:T(8,128)(2,1)}, bf16[2,96,192]{1,2,0:T(8,128)(2,1)}, u32[]{:S(2)}, u32[]{:S(2)}) collective-permute-start(bf16[2,96,192]{1,2,0:T(8,128)(2,1)} %bitcast.215), channel_id=1, source_target_pairs={{0,8},{8,0},{16,24},{24,16},{1,9},{9,1},{17,25},{25,17},{2,10},{10... | collective-permute-start | bytes 221192 | tf_op jit(solution)/shard_map/ppermute | solution.py:55
  306.3 11.3 %collective-permute-start.29 = (bf16[1,96,192]{1,2,0:T(8,128)(2,1)}, bf16[1,96,192]{1,2,0:T(8,128)(2,1)}, u32[]{:S(2)}, u32[]{:S(2)}) collective-permute-start(bf16[1,96,192]{1,2,0:T(8,128)(2,1)} %dynamic-slice_convert_fusion.6), channel_id=1, source_target_pairs={{0,16},{8,24},{16,0},{24,8},{1,17},{9,25},{17,1},{25,9},{2,18},{10... | collective-permute-start | bytes 110600 | tf_op jit(solution)/shard_map/ppermute | solution.py:55
  307.1 29.9 %collective-permute-start.24 = (bf16[4,96,576]{2,1,0:T(8,128)(2,1)}, bf16[4,96,576]{2,1,0:T(8,128)(2,1)}, u32[]{:S(2)}, u32[]{:S(2)}) collective-permute-start(bf16[4,96,576]{2,1,0:T(8,128)(2,1)} %fusion.75), channel_id=1, source_target_pairs={{0,4},{4,0},{1,5},{5,1},{2,6},{6,2},{3,7},{7,3},{8,12},{12,8},{9,1... | collective-permute-start | bytes 1327112 | tf_op jit(solution)/shard_map/ppermute | solution.py:27
  313.6 11.1 %all-to-all-start.8 = ((f32[8,24,96]{2,1,0:T(8,128)}), f32[8,24,96]{2,1,0:T(8,128)}, u32[]{:S(2)}, u32[]{:S(2)}) async-start(f32[8,24,96]{2,1,0:T(8,128)} %bitcast.214), calls=%async_computation.8 | async-start | bytes 196608 | tf_op jit(solution)/shard_map/all_to_all | solution.py:37
  326.9 5.7 %collective-permute-start.19 = (bf16[128,768]{1,0:T(8,128)(2,1)S(1)}, bf16[128,768]{1,0:T(8,128)(2,1)S(1)}, u32[]{:S(2)}, u32[]{:S(2)}) collective-permute-start(bf16[128,768]{1,0:T(8,128)(2,1)S(1)} %slice.337), channel_id=1, source_target_pairs={{0,2},{2,0},{1,3},{3,1},{4,6},{6,4},{5,7},{7,5},{8,10},{10,8},{9,1... | collective-permute-start | bytes 589832 | tf_op jit(solution)/shard_map/ppermute | solution.py:27
  333.7 11.1 %all-to-all-start.7 = ((bf16[8,16,768]{2,1,0:T(8,128)(2,1)}), bf16[8,16,768]{2,1,0:T(8,128)(2,1)S(1)}, u32[]{:S(2)}, u32[]{:S(2)}) async-start(bf16[8,16,768]{2,1,0:T(8,128)(2,1)} %bitcast.37), calls=%async_computation.7 | async-start | bytes 393216 | tf_op jit(solution)/shard_map/all_to_all | solution.py:37
  338.2 12.4 %copy-start.34 = (bf16[8,16,768]{2,1,0:T(8,128)(2,1)S(1)}, bf16[8,16,768]{2,1,0:T(8,128)(2,1)}, u32[]{:S(2)}) copy-start(bf16[8,16,768]{2,1,0:T(8,128)(2,1)} %copy-done.33) | copy-start | bytes 589828
  338.2 12.4 %copy-start.61 = (bf16[128,768]{1,0:T(8,128)(2,1)S(1)}, bf16[128,768]{1,0:T(8,128)(2,1)}, u32[]{:S(2)}) copy-start(bf16[128,768]{1,0:T(8,128)(2,1)} %copy-done.60) | copy-start | bytes 589828
  338.2 12.4 %copy-start.68 = (s32[512]{0:T(512)S(1)}, s32[512]{0:T(512)}, u32[]{:S(2)}) copy-start(s32[512]{0:T(512)} %copy-done.67) | copy-start | bytes 6148
  338.3 8.6 %collective-permute-start.25 = (bf16[2,96,576]{2,1,0:T(8,128)(2,1)S(1)}, bf16[2,96,576]{2,1,0:T(8,128)(2,1)S(1)}, u32[]{:S(2)}, u32[]{:S(2)}) collective-permute-start(bf16[2,96,576]{2,1,0:T(8,128)(2,1)S(1)} %fusion.87), channel_id=1, source_target_pairs={{0,8},{8,0},{16,24},{24,16},{1,9},{9,1},{17,25},{25,17},{2,10},{10... | collective-permute-start | bytes 663560 | tf_op jit(solution)/shard_map/ppermute | solution.py:55
  344.8 5.7 %collective-permute-start.20 = (bf16[128,768]{1,0:T(8,128)(2,1)S(1)}, bf16[128,768]{1,0:T(8,128)(2,1)S(1)}, u32[]{:S(2)}, u32[]{:S(2)}) collective-permute-start(bf16[128,768]{1,0:T(8,128)(2,1)S(1)} %bitcast.206), channel_id=1, source_target_pairs={{0,2},{2,0},{1,3},{3,1},{4,6},{6,4},{5,7},{7,5},{8,10},{10,8},{9,1... | collective-permute-start | bytes 589832 | tf_op jit(solution)/shard_map/ppermute | solution.py:27
  347.0 7.2 %collective-permute-start.26 = (bf16[1,96,576]{2,1,0:T(8,128)(2,1)S(1)}, bf16[1,96,576]{2,1,0:T(8,128)(2,1)S(1)}, u32[]{:S(2)}, u32[]{:S(2)}) collective-permute-start(bf16[1,96,576]{2,1,0:T(8,128)(2,1)S(1)} %dynamic-slice_convert_fusion.5), channel_id=1, source_target_pairs={{0,16},{8,24},{16,0},{24,8},{1,17},{9,25},{17,1},{25,9},{2,18},{10... | collective-permute-start | bytes 331784 | tf_op jit(solution)/shard_map/ppermute | solution.py:55
  350.5 4.4 %collective-permute-start.21 = (bf16[256,768]{1,0:T(8,128)(2,1)S(1)}, bf16[256,768]{1,0:T(8,128)(2,1)S(1)}, u32[]{:S(2)}, u32[]{:S(2)}) collective-permute-start(bf16[256,768]{1,0:T(8,128)(2,1)S(1)} %pad_maximum_fusion.13), channel_id=1, source_target_pairs={{0,1},{1,0},{2,3},{3,2},{4,5},{5,4},{6,7},{7,6},{8,9},{9,8},{10,11... | collective-permute-start | bytes 1179656 | tf_op jit(solution)/shard_map/ppermute | solution.py:27
  (84 other events, 284.5 us)
